TPU v7x, 1024 devices: a whole 4x4x32 slice. The times are simulated.
1024 devices in a mesh: context: 64 (over x, z_hi, y), tensor: 16 (over z_lo, core).
Axes of the slice: x: 4, y: 4, z: 32 (z_hi: 4, z_lo: 8; z = z_hi * 8 + z_lo), core: 2. Of those that a mesh axis runs over, the one named last changes fastest.
Arguments:
- features: bfloat16 [3, 4096, 16384], P(None, 'tensor', 'context'), may hold values from -6 to 6
- short_taps: float32 [3, 3, 4096], P(None, None, 'tensor'), may hold values from -3 to 3
- long_filter: bfloat16 [4096, 16384], P('tensor', 'context'), may hold values from -2 to 2, as said below
- skip_bias: float32 [4096], P('tensor'), may hold values from 0.5 to 1.5
- out_weight: bfloat16 [4096, 4096], P('tensor'), may hold values from -0.125 to 0.125
Outputs:
- layer_out: bfloat16 [16384, 4096], P('context', 'tensor')
Inputs may be any that keep to these rules, and one draw needn't show every extreme that they name: `long_filter`: taps of the implicit filter.
All inputs are finite; a program needn't handle non-finite values.
Results may differ from a plain program's by a relative error of at most 0.007.
Values may be sent and summed in bfloat16 or wider, within the bound.
A program may use at most 32 MiB of HBM per device.

v0:
```python
import math

import jax
import jax.numpy as jnp
from jax import lax
from jax.sharding import PartitionSpec as P


def shifted(value, axis, steps):
    count = lax.axis_size(axis)
    initial, last = (max(0, -steps), min(count, count - steps))
    return lax.ppermute(value, axis, [(source, source + steps) for source in range(initial, last)])


def dft_table(row_count, col_count, modulus):
    row_ids = lax.broadcasted_iota(jnp.int32, (row_count, col_count), 0)
    col_ids = lax.broadcasted_iota(jnp.int32, (row_count, col_count), 1)
    angle = (row_ids * col_ids % modulus).astype(jnp.float32) * (2.0 * math.pi / modulus)
    return (jnp.cos(angle), jnp.sin(angle))


def split_length(size):
    first = 2
    for cand in range(2, int(math.isqrt(size)) + 1, 2):
        if size % cand == 0:
            first = cand
    return (first, size // first)


def long_conv(kv_part, filter_part, bias_part):
    channel_count, total = kv_part.shape
    size = 2 * total
    first, second = split_length(size)
    half = first // 2
    level = lax.Precision.HIGH
    cos_one, sin_one = dft_table(first, first, first)
    twid_cos, twid_sin = dft_table(first, second, size)
    cos_two, sin_two = dft_table(second, second, second)
    kv_float = kv_part.astype(jnp.float32)
    stacked = jnp.concatenate([kv_float, filter_part.astype(jnp.float32)], axis=0)
    blocked = stacked.reshape(2 * channel_count, half, second)
    a_real = jnp.einsum("kn,cnm->ckm", cos_one[:, :half], blocked, precision=level)
    a_imag = -jnp.einsum("kn,cnm->ckm", sin_one[:, :half], blocked, precision=level)
    b_real = a_real * twid_cos + a_imag * twid_sin
    b_imag = a_imag * twid_cos - a_real * twid_sin
    c_real = jnp.einsum("ckm,mj->ckj", b_real, cos_two, precision=level) + jnp.einsum(
        "ckm,mj->ckj", b_imag, sin_two, precision=level
    )
    c_imag = jnp.einsum("ckm,mj->ckj", b_imag, cos_two, precision=level) - jnp.einsum(
        "ckm,mj->ckj", b_real, sin_two, precision=level
    )
    z_real, h_real = (c_real[:channel_count], c_real[channel_count:])
    z_imag, h_imag = (c_imag[:channel_count], c_imag[channel_count:])
    y_real = z_real * h_real - z_imag * h_imag
    y_imag = z_real * h_imag + z_imag * h_real
    g_real = jnp.einsum("ckj,jm->ckm", y_real, cos_two, precision=level) - jnp.einsum(
        "ckj,jm->ckm", y_imag, sin_two, precision=level
    )
    g_imag = jnp.einsum("ckj,jm->ckm", y_imag, cos_two, precision=level) + jnp.einsum(
        "ckj,jm->ckm", y_real, sin_two, precision=level
    )
    t_real = g_real * twid_cos - g_imag * twid_sin
    t_imag = g_imag * twid_cos + g_real * twid_sin
    output = jnp.einsum("nk,ckm->cnm", cos_one[:half, :], t_real, precision=level) - jnp.einsum(
        "nk,ckm->cnm", sin_one[:half, :], t_imag, precision=level
    )
    output = output.reshape(channel_count, total) / size
    return output + bias_part[:, None] * kv_float


def local(features, short_taps, long_filter, skip_bias, out_weight):
    seq_len = features.shape[2]
    local_channels = features.shape[1]
    rim = shifted(features[:, :, seq_len - 2 :], "context", 1)
    extended = jnp.concatenate([rim, features], axis=2).astype(jnp.float32)
    shaped = (
        short_taps[:, 0, :, None] * extended[:, :, 2:]
        + short_taps[:, 1, :, None] * extended[:, :, 1:-1]
        + short_taps[:, 2, :, None] * extended[:, :, :-2]
    )
    gate = shaped[0].astype(jnp.bfloat16)
    kv_product = (shaped[1] * shaped[2]).astype(jnp.bfloat16)
    per_device = local_channels // lax.axis_size("context")
    bias_part = lax.dynamic_slice_in_dim(
        skip_bias, lax.axis_index("context") * per_device, per_device, 0
    )
    kv_cols, filter_cols, gate_cols = (
        lax.all_to_all(kv_product, "context", split_axis=0, concat_axis=1, tiled=True),
        lax.all_to_all(long_filter, "context", split_axis=0, concat_axis=1, tiled=True),
        lax.all_to_all(gate, "context", split_axis=0, concat_axis=1, tiled=True),
    )
    mixed = lax.optimization_barrier(
        long_conv(kv_cols, filter_cols, bias_part).astype(jnp.bfloat16)
    )
    gated_cols = (gate_cols.astype(jnp.float32) * mixed.astype(jnp.float32)).astype(jnp.bfloat16)
    gated = lax.all_to_all(gated_cols, "context", split_axis=1, concat_axis=0, tiled=True)
    partial_out = lax.dot_general(
        gated, out_weight, (((0,), (0,)), ((), ())), preferred_element_type=jnp.float32
    )
    summed = lax.psum_scatter(partial_out, "tensor", scatter_dimension=1, tiled=True)
    return summed.astype(jnp.bfloat16)


def solution(mesh):
    placed = (
        P(None, "tensor", "context"),
        P(None, None, "tensor"),
        P("tensor", "context"),
        P("tensor"),
        P("tensor", None),
    )
    return jax.shard_map(
        local, mesh=mesh, in_specs=placed, out_specs=P("context", "tensor"), check_vma=False
    )
```

profile of v0, /device:TPU:24, one launch (start us, length us, event | category | flops | bytes accessed | tf_op | source)
XLA Modules:
  0.0 323.7 jit_solution(8966898020957232288)
XLA Ops:
  6.5 0.0 copy-start
  6.5 1.2 slice.56
  7.7 15.4 %collective-permute-start = (bf16[3,256,2]{2,1,0:T(8,128)(2,1)S(1)}, bf16[3,256,2]{2,1,0:T(8,128)(2,1)S(1)}, u32[]{:S(2)}, u32[]{:S(2)}) collective-permute-start(bf16[3,256,2]{2,1,0:T(8,128)(2,1)S(1)} %slice.56), channel_id=1, source_target_pairs={{0,16},{16,32},{32,48},{48,64},{64,80},{80,96},{96,112},{112,128},... | collective-permute-start | bytes 9224 | tf_op jit(solution)/shard_map/ppermute | solution.py:12
  23.1 1.6 all_to_all.42
  24.7 24.4 %all-to-all-start.2 = ((bf16[64,4,256]{2,1,0:T(4,128)(2,1)}), bf16[64,4,256]{2,1,0:T(4,128)(2,1)S(1)}, u32[]{:S(2)}, u32[]{:S(2)}) async-start(bf16[64,4,256]{2,1,0:T(4,128)(2,1)} %all_to_all.42), calls=%async_computation.2 | async-start | bytes 262144 | tf_op jit(solution)/shard_map/all_to_all | solution.py:89
  49.2 0.8 fusion.95
  50.0 0.0 collective-permute-done
  50.0 1.3 maximum_convert_fusion
  51.3 0.0 copy-start.3
  51.3 0.8 fusion.3
  52.1 0.7 convert_element_type.108
  52.8 34.4 %all-to-all-done.2 = bf16[64,4,256]{2,1,0:T(4,128)(2,1)S(1)} async-done(((bf16[64,4,256]{2,1,0:T(4,128)(2,1)}), bf16[64,4,256]{2,1,0:T(4,128)(2,1)S(1)}, u32[]{:S(2)}, u32[]{:S(2)}) %all-to-all-start.2) | async-done | bytes 131104 | tf_op jit(solution)/shard_map/all_to_all | solution.py:89
  87.2 13.3 %all-to-all-start.1 = ((bf16[64,4,256]{2,1,0:T(4,128)(2,1)}), bf16[64,4,256]{2,1,0:T(4,128)(2,1)}, u32[]{:S(2)}, u32[]{:S(2)}) async-start(bf16[64,4,256]{2,1,0:T(4,128)(2,1)} %convert_element_type.108), calls=%async_computation.1 | async-start | bytes 262144 | tf_op jit(solution)/shard_map/all_to_all | solution.py:88
  100.6 0.5 fusion.54
  101.1 0.1 copy.31
  101.2 0.1 copy.30
  101.3 0.0 copy-done.3
  101.3 0.1 dynamic_slice.3
  101.4 0.9 fusion.60
  102.3 0.9 fusion.59
  103.2 0.7 slice.119
  103.8 0.0 copy-start.2
  103.8 1.6 convert_element_type.103
  105.5 20.2 %all-to-all-done.1 = bf16[64,4,256]{2,1,0:T(4,128)(2,1)} async-done(((bf16[64,4,256]{2,1,0:T(4,128)(2,1)}), bf16[64,4,256]{2,1,0:T(4,128)(2,1)}, u32[]{:S(2)}, u32[]{:S(2)}) %all-to-all-start.1) | async-done | bytes 131104 | tf_op jit(solution)/shard_map/all_to_all | solution.py:88
  125.7 9.0 %all-to-all-start = ((bf16[64,4,256]{2,1,0:T(4,128)(2,1)}), bf16[64,4,256]{2,1,0:T(4,128)(2,1)S(1)}, u32[]{:S(2)}, u32[]{:S(2)}) async-start(bf16[64,4,256]{2,1,0:T(4,128)(2,1)} %convert_element_type.103), calls=%async_computation | async-start | bytes 262144 | tf_op jit(solution)/shard_map/all_to_all | solution.py:90
  134.7 0.2 reduce-scatter.2.cloned.1.call-start
  134.9 0.9 convert_bitcast_fusion
  135.9 1.3 convolution_bitcast_fusion
  137.2 0.0 copy-done.2
  137.2 0.5 fusion
  137.7 1.9 fusion.24
  139.6 1.9 fusion.26
  141.5 1.9 convolution_subtract_fusion
  143.4 1.9 convolution_add_fusion
  145.3 0.1 multiply_subtract_fusion.1
  145.5 1.3 fusion.20
  146.8 0.0 copy-start.1
  146.8 1.3 fusion.22
  148.2 1.6 convolution_add_fusion.1
  149.8 1.4 convolution_subtract_fusion.1
  151.1 0.0 copy-done.1
  151.1 0.3 fusion.8
  151.5 0.3 fusion.2
  151.8 0.2 copy.45
  152.0 0.2 copy.46
  152.2 0.1 add_convert_fusion
  152.3 7.6 %all-to-all-done = bf16[64,4,256]{2,1,0:T(4,128)(2,1)S(1)} async-done(((bf16[64,4,256]{2,1,0:T(4,128)(2,1)}), bf16[64,4,256]{2,1,0:T(4,128)(2,1)S(1)}, u32[]{:S(2)}, u32[]{:S(2)}) %all-to-all-start) | async-done | bytes 131104 | tf_op jit(solution)/shard_map/all_to_all | solution.py:90
  159.9 0.1 multiply_convert_fusion
  160.0 44.5 %all_to_all.52 = bf16[4,64,256]{2,0,1:T(4,128)(2,1)S(1)} all-to-all(bf16[4,64,256]{2,0,1:T(4,128)(2,1)S(1)} %bitcast.72), channel_id=1, replica_groups=mesh['context'=64,'tensor'=16] {'context'}, dimensions={1} | all-to-all | bytes 262144 | tf_op jit(solution)/shard_map/all_to_all | solution.py:96
  204.6 0.0 copy-done
  204.6 2.7 fusion.96
  207.3 0.0 reduce-scatter.2.cloned.1.call-update
  207.3 107.9 %reduce-scatter.2.cloned.1.call-done = f32[256,256]{1,0:T(8,128)} async-done(((f32[256,4096]{1,0:T(8,128)}), f32[256,256]{1,0:T(8,128)}) %reduce-scatter.2.cloned.1.call-update) | async-done | bytes 262160 | tf_op jit(solution)/shard_map/reduce_scatter | solution.py:100
  315.3 1.6 convert_element_type.119
  (6 shorter events, 0.1 us)
Async XLA Ops:
  6.5 198.1 %copy-start = (bf16[256,4096]{1,0:T(8,128)(2,1)S(1)}, bf16[256,4096]{1,0:T(8,128)(2,1)}, u32[]{:S(2)}) copy-start(bf16[256,4096]{1,0:T(8,128)(2,1)} %param.9) | copy-start | bytes 6291460
  7.7 42.3 %collective-permute-start = (bf16[3,256,2]{2,1,0:T(8,128)(2,1)S(1)}, bf16[3,256,2]{2,1,0:T(8,128)(2,1)S(1)}, u32[]{:S(2)}, u32[]{:S(2)}) collective-permute-start(bf16[3,256,2]{2,1,0:T(8,128)(2,1)S(1)} %slice.56), channel_id=1, source_target_pairs={{0,16},{16,32},{32,48},{48,64},{64,80},{80,96},{96,112},{112,128},... | collective-permute-start | bytes 9224 | tf_op jit(solution)/shard_map/ppermute | solution.py:12
  24.7 62.5 %all-to-all-start.2 = ((bf16[64,4,256]{2,1,0:T(4,128)(2,1)}), bf16[64,4,256]{2,1,0:T(4,128)(2,1)S(1)}, u32[]{:S(2)}, u32[]{:S(2)}) async-start(bf16[64,4,256]{2,1,0:T(4,128)(2,1)} %all_to_all.42), calls=%async_computation.2 | async-start | bytes 262144 | tf_op jit(solution)/shard_map/all_to_all | solution.py:89
  51.3 50.0 %copy-start.3 = (f32[256]{0:T(256)S(1)}, f32[256]{0:T(256)}, u32[]{:S(2)}) copy-start(f32[256]{0:T(256)} %param.8) | copy-start | bytes 3076
  87.2 38.4 %all-to-all-start.1 = ((bf16[64,4,256]{2,1,0:T(4,128)(2,1)}), bf16[64,4,256]{2,1,0:T(4,128)(2,1)}, u32[]{:S(2)}, u32[]{:S(2)}) async-start(bf16[64,4,256]{2,1,0:T(4,128)(2,1)} %convert_element_type.108), calls=%async_computation.1 | async-start | bytes 262144 | tf_op jit(solution)/shard_map/all_to_all | solution.py:88
  103.8 33.3 %copy-start.2 = (f32[128,128]{0,1:T(8,128)S(1)}, f32[128,128]{0,1:T(8,128)}, u32[]{:S(2)}) copy-start(f32[128,128]{0,1:T(8,128)} %fusion.59) | copy-start | bytes 196612
  125.7 34.3 %all-to-all-start = ((bf16[64,4,256]{2,1,0:T(4,128)(2,1)}), bf16[64,4,256]{2,1,0:T(4,128)(2,1)S(1)}, u32[]{:S(2)}, u32[]{:S(2)}) async-start(bf16[64,4,256]{2,1,0:T(4,128)(2,1)} %convert_element_type.103), calls=%async_computation | async-start | bytes 262144 | tf_op jit(solution)/shard_map/all_to_all | solution.py:90
  134.7 180.6 %reduce-scatter.2.cloned.1.call-start = ((), (), s32[]{:S(2)}) async-start(), calls=%async_computation.5 | async-start | bytes 4456448 | tf_op jit(solution)/shard_map/reduce_scatter | solution.py:100
  146.8 4.3 %copy-start.1 = (f32[128,128]{0,1:T(8,128)S(1)}, f32[128,128]{0,1:T(8,128)}, u32[]{:S(2)}) copy-start(f32[128,128]{0,1:T(8,128)} %fusion.60) | copy-start | bytes 196612
Sparse Core Ops, SparseCore 0:
  207.5 107.7 reduce-scatter.1
where the time goes:
time: 325 us; the launch traced here: 324 us
  waiting for transfers between devices  170 us (52%)
  starting transfers between devices  62.4 us (19%)
  blocking collectives  44.5 us (14%)
  matrix products  18.4 us (6%)
  between operations  13.7 us (4%)
  other arithmetic  7.29 us (2%)
  local copies, waits for them, and re-layouts  7.28 us (2%)
    reduce_scatter x1, waiting for transfers between devices, local(): lax.psum_scatter(partial_out, 'tensor', scatter_dimension=1, tiled=True)  108 us
    all_to_all x1, blocking collectives, local(): lax.all_to_all(gated_cols, 'context', split_axis=1, concat_axis=0, tiled=...  44.5 us
    all_to_all x1, waiting for transfers between devices, local(): lax.all_to_all(long_filter, 'context', split_axis=0, concat_axis=1, tiled...  34.4 us
    all_to_all x1, starting transfers between devices, local(): lax.all_to_all(long_filter, 'context', split_axis=0, concat_axis=1, tiled...  24.4 us
    all_to_all x1, waiting for transfers between devices, local(): lax.all_to_all(kv_product, 'context', split_axis=0, concat_axis=1, tiled=...  20.2 us
    ppermute x1, starting transfers between devices, shifted(): lax.ppermute(value, axis, [(source, source + steps) for source in range(i...  15.4 us
    all_to_all x1, starting transfers between devices, local(): lax.all_to_all(kv_product, 'context', split_axis=0, concat_axis=1, tiled=...  13.3 us
    all_to_all x1, starting transfers between devices, local(): lax.all_to_all(gate, 'context', split_axis=0, concat_axis=1, tiled=True)  9.04 us
  transfers between devices with their start and end apart: 5, of which 4 were waited for; matrix products, arithmetic and copies ran while one was open for 8% of the time, Pallas kernels for 0%

commit v1 on v0

v1 whole, which is shorter than its diff:
```python
import jax
import jax.numpy as jnp
from jax import lax
from jax.experimental import pallas as pl
from jax.experimental.pallas import tpu as pltpu
from jax.sharding import PartitionSpec as P

MESH = pl.DeviceIdType.MESH
F32 = jnp.float32
BF16 = jnp.bfloat16
SIDE = 256
LANES = 128
PARTS = 4
LAG = 4
STEPS = 7 * PARTS


def remote(src, dst, send_sem, recv_sem, device):
    return pltpu.make_async_remote_copy(
        src_ref=src, dst_ref=dst, send_sem=send_sem, recv_sem=recv_sem,
        device_id=device, device_id_type=MESH,
    )


def kernel(
    feat_hbm, taps_ref, filt_hbm, bias_ref, w_hbm, out_ref,
    feat, filt, w, cols, halo_out, halo_in, bias_in, gate, kv,
    filt_xy, filt_zs, filt_zr, kv_xy, kv_zs, kv_zr,
    mix_zs, mix_zr, mix_ss, mix,
    turn, hpad, xpad, ypad, piece, xs_buf, toep, gated_t,
    sib_out, sib_in, own, right_out, right_in, left_out, left_in,
    load_sem, halo_sem, bias_sem,
    xy_send, xy_recv, z_send, z_recv, back_send, back_recv,
    sib_send, sib_recv, right_send, right_recv, left_send, left_recv,
):
    context = lax.axis_index("context")
    tensor = lax.axis_index("tensor")
    here = (context // 16) * 4 + context % 4
    z_hi = (context // 4) % 4
    z_lo = tensor // 2
    core = tensor % 2

    def plane(place):
        return ((place // 4) * 16 + z_hi * 4 + place % 4, tensor)

    def across(target_hi):
        return (
            (context // 16) * 16 + target_hi * 4 + context % 4,
            ((z_lo + 4) % 8) * 2 + core,
        )

    after = ((context + 1) % 64, tensor)
    before = ((context + 63) % 64, tensor)
    sibling = (context, z_lo * 2 + 1 - core)
    right = (context, ((z_lo + 1) % 8) * 2 + core)
    left = (context, ((z_lo + 7) % 8) * 2 + core)

    loads = [
        pltpu.make_async_copy(feat_hbm, feat, load_sem.at[0]),
        pltpu.make_async_copy(filt_hbm, filt, load_sem.at[1]),
        pltpu.make_async_copy(w_hbm, w, load_sem.at[2]),
    ]
    for load in loads:
        load.start()

    barrier = pltpu.get_barrier_semaphore()
    peers = [plane((here + step) % 16) for step in range(1, 16)]
    peers += [across((z_hi + step) % 4) for step in range(4)]
    peers += [before, sibling, right, left]
    for peer in peers:
        pl.semaphore_signal(barrier, inc=1, device_id=peer, device_id_type=MESH)

    loads[0].wait()
    loads[1].wait()

    row = lax.broadcasted_iota(jnp.int32, (16, SIDE), 0)
    pos = lax.broadcasted_iota(jnp.int32, (16, SIDE), 1)
    edge = jnp.zeros((16, SIDE), F32)
    for stream in range(3):
        pick = ((row - 2 * stream == pos - (SIDE - 2)) & (pos >= SIDE - 2)).astype(F32).astype(BF16)
        edge = edge + lax.dot_general(
            pick, feat[stream], (((1,), (1,)), ((), ())), preferred_element_type=F32
        )
    halo_out[...] = edge.astype(BF16)
    cols[...] = jnp.zeros((LANES, SIDE), F32)
    for stream in range(3):
        for tap in range(3):
            cols[pl.ds(3 * stream + tap, 1), :] = taps_ref[stream, pl.ds(tap, 1), :]
    hpad[:, 0:8, :] = jnp.zeros((4, 8, LANES), F32)
    xpad[:, 0:16, :] = jnp.zeros((4, 16, LANES), F32)

    pl.semaphore_wait(barrier, len(peers))

    halo_copy = remote(halo_out, halo_in, halo_sem.at[0], halo_sem.at[1], after)
    halo_copy.start()
    bias_copy = remote(bias_ref, bias_in, bias_sem.at[0], bias_sem.at[1], across(z_hi))
    bias_copy.start()

    sent = [halo_copy, bias_copy]

    def plane_exchange(src, dst, which):
        copies = []
        for step in range(1, 16):
            to = (here + step) % 16
            copy = remote(
                src.at[pl.ds(pl.multiple_of(to * 16, 16), 16)],
                dst.at[pl.ds(pl.multiple_of(here * 16, 16), 16)],
                xy_send.at[which, step], xy_recv.at[which, step], plane(to),
            )
            copy.start()
            copies.append(copy)
        mine = pl.ds(pl.multiple_of(here * 16, 16), 16)
        dst[mine, :] = src[mine, :]
        sent.extend(copies)
        return copies

    def across_exchange(src, dst, which):
        copies = []
        for step in (2, 1, 3, 0):
            to = (z_hi + step) % 4
            copy = remote(
                src.at[pl.ds(pl.multiple_of(to * 64, 64), 64)],
                dst.at[pl.ds(pl.multiple_of(z_hi * 64, 64), 64)],
                z_send.at[which, step], z_recv.at[which, step], across(to),
            )
            copy.start()
            copies.append(copy)
        sent.extend(copies)
        return copies

    def arrived(copies):
        for copy in copies:
            copy.wait_recv()

    def swap_blocks(src, dst):
        for half in range(2):
            lanes = pl.ds(half * LANES, LANES)
            turn[half] = src[:, lanes].astype(F32)
        for j in range(16):
            for half in range(2):
                block = turn[half, pl.ds(j, 16, stride=16), :]
                dst[pl.ds(16 * j, 16), pl.ds(half * LANES, LANES)] = block.astype(BF16)

    def spread(src, dst, ahead):
        for zs in range(4):
            for ch in range(4):
                tile = src[pl.ds(zs * 64 + ch * 16, 16), :].astype(F32)
                for xs in range(4):
                    for half in range(2):
                        first = ahead + (xs * 16 + zs * 4) * 2 + half
                        dst[ch, pl.ds(first, 4, stride=2), :] = tile[
                            4 * xs : 4 * xs + 4, half * LANES : (half + 1) * LANES
                        ]

    filt_plane = plane_exchange(filt, filt_xy, 0)
    arrived(filt_plane)
    swap_blocks(filt_xy, filt_zs)
    filt_across = across_exchange(filt_zs, filt_zr, 0)

    halo_copy.wait_recv()
    seen = jnp.where(context > 0, 1.0, 0.0)
    cols[16:32, :] = halo_in[...].astype(F32) * seen
    turned = cols[...].T
    lane = lax.broadcasted_iota(jnp.int32, (64, SIDE), 1)
    for block in range(4):
        rows = slice(64 * block, 64 * block + 64)
        shaped = []
        for stream in range(3):
            now = feat[stream, rows, :].astype(F32)
            last = turned[rows, 16 + 2 * stream + 1 : 16 + 2 * stream + 2]
            older = turned[rows, 16 + 2 * stream : 16 + 2 * stream + 1]
            one = jnp.where(lane == 0, last, pltpu.roll(now, 1, 1))
            two = jnp.where(lane == 0, older, jnp.where(lane == 1, last, pltpu.roll(now, 2, 1)))
            tap = [turned[rows, 3 * stream + j : 3 * stream + j + 1] for j in range(3)]
            shaped.append(tap[0] * now + tap[1] * one + tap[2] * two)
        gate[rows, :] = shaped[0].astype(BF16)
        kv[rows, :] = (shaped[1] * shaped[2]).astype(BF16)

    kv_plane = plane_exchange(kv, kv_xy, 1)
    arrived(kv_plane)
    swap_blocks(kv_xy, kv_zs)
    kv_across = across_exchange(kv_zs, kv_zr, 1)

    arrived(filt_across)
    spread(filt_zr, hpad, 8)

    lower = lax.broadcasted_iota(jnp.int32, (LANES, LANES), 1)
    upper = lax.broadcasted_iota(jnp.int32, (LANES, LANES), 0)
    keep = lower + upper < LANES

    def build(index, carry):
        ch = index // 16
        b = index % 16
        for a in range(8):
            now = hpad[ch, pl.ds(8 + 16 * a + b, 1), :]
            past = hpad[ch, pl.ds(7 + 16 * a + b, 1), :]
            block = jnp.where(
                keep,
                jnp.broadcast_to(now, (LANES, LANES)),
                jnp.broadcast_to(past, (LANES, LANES)),
            )
            block = pltpu.roll(block, 0, 1, stride=1, stride_axis=0)
            toep[ch, pl.ds(pl.multiple_of(b * LANES, LANES), LANES), pl.ds(a * LANES, LANES)] = (
                block.astype(BF16)
            )
        return carry

    lax.fori_loop(0, 64, build, 0)

    bias_copy.wait_recv()
    arrived(kv_across)
    spread(kv_zr, xpad, 16)

    back = []
    for ch in range(4):
        for b in range(16):
            xs_buf[:, pl.ds(b * LANES, LANES)] = xpad[ch, pl.ds(16 - b, LANES), :].astype(BF16)
        total = None
        for a in range(4):
            part = jnp.dot(
                xs_buf[pl.ds(0, LANES - 32 * a), :],
                toep[ch, :, pl.ds(2 * a * LANES, 2 * LANES)],
                preferred_element_type=F32,
            )
            low, high = part[:, :LANES], part[: LANES - 32 * a - 16, LANES:]
            if a:
                low = jnp.concatenate([jnp.zeros((32 * a, LANES), F32), low], axis=0)
            high = jnp.concatenate([jnp.zeros((32 * a + 16, LANES), F32), high], axis=0)
            total = low + high if total is None else total + low + high
        channel = here * 16 + z_hi * 4 + ch
        spot = lax.broadcasted_iota(jnp.int32, (1, SIDE), 1)
        bias = jnp.sum(jnp.where(spot == channel, bias_in[...], 0.0), axis=1, keepdims=True)
        ypad[...] = total + bias * xpad[ch, pl.ds(16, LANES), :]
        for zs in range(4):
            for xs in range(4):
                for half in range(2):
                    first = (xs * 16 + zs * 4) * 2 + half
                    piece[pl.ds(4 * xs, 4), pl.ds(half * LANES, LANES)] = ypad[
                        pl.ds(first, 4, stride=2), :
                    ]
            mix_zs[pl.ds(zs * 64 + ch * 16, 16), :] = piece[...].astype(BF16)
        for step in (2, 1, 3, 0):
            to = (z_hi + step) % 4
            copy = remote(
                mix_zs.at[pl.ds(pl.multiple_of(to * 64 + ch * 16, 16), 16)],
                mix_zr.at[pl.ds(pl.multiple_of(z_hi * 64 + ch * 16, 16), 16)],
                back_send.at[ch, step], back_recv.at[ch, step], across(to),
            )
            copy.start()
            back.append(copy)
    sent.extend(back)

    arrived(back)
    swap_blocks(mix_zr, mix_ss)
    arrived(plane_exchange(mix_ss, mix, 2))

    gated = (gate[...].astype(F32) * mix[...].astype(F32)).astype(BF16).astype(F32)
    gated_t[...] = gated.T.astype(BF16)
    loads[2].wait()

    def sib_copy(d):
        return remote(sib_out.at[d], sib_in.at[d], sib_send.at[d], sib_recv.at[d], sibling)

    for d in (7, 0, 6, 1, 5, 2, 4, 3):
        theirs = pl.ds(pl.multiple_of((2 * d + 1 - core) * SIDE, SIDE), SIDE)
        mine = pl.ds(pl.multiple_of((2 * d + core) * SIDE, SIDE), SIDE)
        sib_out[d] = jnp.dot(gated_t[...], w[:, theirs], preferred_element_type=F32).astype(BF16)
        sib_copy(d).start()
        own[d] = jnp.dot(gated_t[...], w[:, mine], preferred_element_type=F32)

    size = SIDE // PARTS

    def rows_of(n):
        return pl.ds(pl.multiple_of((n % PARTS) * size, size), size)

    def right_copy(n):
        d = 7 - n // PARTS
        return remote(
            right_out.at[d, rows_of(n)], right_in.at[d, rows_of(n)],
            right_send.at[n], right_recv.at[n], right,
        )

    def left_copy(n):
        d = n // PARTS
        return remote(
            left_out.at[d, rows_of(n)], left_in.at[d, rows_of(n)],
            left_send.at[n], left_recv.at[n], left,
        )

    def pass_on(n, d, first, copy, came, going):
        rows = rows_of(n)

        @pl.when(n % PARTS == 0)
        def _():
            sib_copy(d).wait_recv()

        @pl.when(first)
        def _():
            going[d, rows, :] = (own[d, rows, :] + sib_in[d, rows, :].astype(F32)).astype(BF16)

        @pl.when(jnp.logical_not(first))
        def _():
            copy.wait_recv()
            going[d, rows, :] = (
                own[d, rows, :] + sib_in[d, rows, :].astype(F32) + came[d, rows, :].astype(F32)
            ).astype(BF16)

        copy.start()

    def reduce_step(moment, carry):
        n = moment - z_lo * LAG

        @pl.when((n >= 0) & (n < (7 - z_lo) * PARTS))
        def _():
            pass_on(n, 7 - n // PARTS, z_lo == 0, right_copy(n), right_in, right_out)

        m = moment - (7 - z_lo) * LAG

        @pl.when((m >= 0) & (m < z_lo * PARTS))
        def _():
            pass_on(m, m // PARTS, z_lo == 7, left_copy(m), left_in, left_out)

        return carry

    lax.fori_loop(0, STEPS + 6 * LAG, reduce_step, 0)

    sib_copy(z_lo).wait_recv()
    own[z_lo] = own[z_lo] + sib_in[z_lo].astype(F32)

    @pl.when(z_lo > 0)
    def _():
        for part in range(PARTS):
            n = (7 - z_lo) * PARTS + part
            right_copy(n).wait_recv()
        own[z_lo] = own[z_lo] + right_in[z_lo].astype(F32)

    @pl.when(z_lo < 7)
    def _():
        for part in range(PARTS):
            n = z_lo * PARTS + part
            left_copy(n).wait_recv()
        own[z_lo] = own[z_lo] + left_in[z_lo].astype(F32)

    out_ref[...] = own[z_lo].astype(BF16)

    for copy in sent:
        copy.wait_send()
    for d in range(8):
        sib_copy(d).wait_send()

    def close(n, carry):
        @pl.when(n < (7 - z_lo) * PARTS)
        def _():
            right_copy(n).wait_send()

        @pl.when(n < z_lo * PARTS)
        def _():
            left_copy(n).wait_send()

        return carry

    lax.fori_loop(0, STEPS, close, 0)


def local(features, short_taps, long_filter, skip_bias, out_weight):
    vmem = pl.BlockSpec(memory_space=pltpu.VMEM)
    anywhere = pl.BlockSpec(memory_space=pl.ANY)
    square = pltpu.VMEM((SIDE, SIDE), BF16)
    dma = pltpu.SemaphoreType.DMA
    return pl.pallas_call(
        kernel,
        out_shape=jax.ShapeDtypeStruct((SIDE, SIDE), BF16),
        in_specs=[anywhere, vmem, anywhere, vmem, anywhere],
        out_specs=vmem,
        scratch_shapes=[
            pltpu.VMEM((3, SIDE, SIDE), BF16),
            square,
            pltpu.VMEM((SIDE, 16 * SIDE), BF16),
            pltpu.VMEM((LANES, SIDE), F32),
            pltpu.VMEM((16, SIDE), BF16),
            pltpu.VMEM((16, SIDE), BF16),
            pltpu.VMEM((1, SIDE), F32),
            square, square,
            square, square, square,
            square, square, square,
            square, square, square, square,
            pltpu.VMEM((2, SIDE, LANES), F32),
            pltpu.VMEM((4, 136, LANES), F32),
            pltpu.VMEM((4, 144, LANES), F32),
            pltpu.VMEM((LANES, LANES), F32),
            pltpu.VMEM((16, SIDE), F32),
            pltpu.VMEM((LANES, 2048), BF16),
            pltpu.VMEM((4, 2048, 1024), BF16),
            square,
            pltpu.VMEM((8, SIDE, SIDE), BF16),
            pltpu.VMEM((8, SIDE, SIDE), BF16),
            pltpu.VMEM((8, SIDE, SIDE), F32),
            pltpu.VMEM((8, SIDE, SIDE), BF16),
            pltpu.VMEM((8, SIDE, SIDE), BF16),
            pltpu.VMEM((8, SIDE, SIDE), BF16),
            pltpu.VMEM((8, SIDE, SIDE), BF16),
            dma((3,)), dma((2,)), dma((2,)),
            dma((3, 16)), dma((3, 16)),
            dma((2, 4)), dma((2, 4)),
            dma((4, 4)), dma((4, 4)),
            dma((8,)), dma((8,)),
            dma((STEPS,)), dma((STEPS,)), dma((STEPS,)), dma((STEPS,)),
        ],
        compiler_params=pltpu.CompilerParams(
            collective_id=0, has_side_effects=True, vmem_limit_bytes=50 << 20
        ),
        cost_estimate=pl.CostEstimate(
            flops=4 * 10**9, bytes_accessed=3 * 10**6, transcendentals=0
        ),
        name="hyena_operator",
    )(features, short_taps, long_filter, skip_bias.reshape(1, SIDE), out_weight)


def solution(mesh):
    placed = (
        P(None, "tensor", "context"),
        P(None, None, "tensor"),
        P("tensor", "context"),
        P("tensor"),
        P("tensor", None),
    )
    return jax.shard_map(
        local, mesh=mesh, in_specs=placed, out_specs=P("context", "tensor"), check_vma=False
    )
```

time: 325 us -> 118 us (0.36)
  waiting for transfers between devices: 170 us -> 0 us
  Pallas kernels: 0 us -> 112 us
  starting transfers between devices: 62.4 us -> 0 us
  blocking collectives: 44.5 us -> 0 us
  matrix products: 18.4 us -> 0 us
  between operations: 13.7 us -> 0.01 us
  other arithmetic: 7.29 us -> 0 us
    pallas_call x0 -> x1, Pallas kernels: none -> 112 us  [local(): pl.pallas_call(kernel, out_shape=jax.ShapeDtypeStruct((SIDE, SIDE), BF16)...]
    reduce_scatter x1 -> x0, waiting for transfers between devices: 108 us -> none  [local(): lax.psum_scatter(partial_out, 'tensor', scatter_dimension=1, tiled=True)]
    all_to_all x3 -> x0, waiting for transfers between devices: 62.2 us -> none  [the longest x1 34.4 us: local(): lax.all_to_all(long_filter, 'context', split_axis=0, concat_axis=1, tiled...]
    all_to_all x3 -> x0, starting transfers between devices: 46.8 us -> none  [the longest x1 24.4 us: local(): lax.all_to_all(long_filter, 'context', split_axis=0, concat_axis=1, tiled...]
    all_to_all x1 -> x0, blocking collectives: 44.5 us -> none  [local(): lax.all_to_all(gated_cols, 'context', split_axis=1, concat_axis=0, tiled=...]
    dot_general x13 -> x0, matrix products: 18.4 us -> none  [the longest x1 2.7 us: local(): lax.dot_general(gated, out_weight, (((0,), (0,)), ((), ())), preferred_el...]
    ppermute x1 -> x0, starting transfers between devices: 15.4 us -> none  [shifted(): lax.ppermute(value, axis, [(source, source + steps) for source in range(i...]
    unnamed x12 -> x11, local copies, waits for them, and re-layouts: 0.37 us -> 5.53 us
  transfers between devices with their start and end apart: 5 -> 0, of which waited for: 4 -> 0; matrix products, arithmetic and copies ran while one was open for 8% -> 0% of each run, Pallas kernels for 0% -> 0%
where the time goes in v1:
time: 118 us; the launch traced here: 117 us
  Pallas kernels  112 us (95%)
  local copies, waits for them, and re-layouts  5.53 us (5%)
    pallas_call x1, Pallas kernels, local(): pl.pallas_call(kernel, out_shape=jax.ShapeDtypeStruct((SIDE, SIDE), BF16)...  112 us
    unnamed x11, local copies, waits for them, and re-layouts  5.53 us

profile of v1, /device:TPU:24, one launch (start us, length us, event | category | flops | bytes accessed | tf_op | source)
XLA Modules:
  0.0 117.3 jit_solution(6053784507926485874)
XLA Ops:
  0.0 0.0 copy-start
  0.0 1.6 %copy-done = bf16[256,4096]{1,0:T(8,128)(2,1)S(1)} copy-done((bf16[256,4096]{1,0:T(8,128)(2,1)S(1)}, bf16[256,4096]{1,0:T(8,128)(2,1)}, u32[]{:S(2)}) %copy-start) | copy-done | bytes 2097176
  1.6 0.0 copy-start.1
  1.6 1.0 copy-done.1
  2.6 0.0 copy-start.2
  2.6 0.9 copy-done.2
  3.5 0.0 copy-start.3
  3.5 0.7 copy-done.3
  4.2 0.0 copy-start.4
  4.2 0.7 copy-done.4
  4.9 111.7 %hyena_operator.1 = bf16[256,256]{1,0:T(8,128)(2,1)S(1)} custom-call(bf16[3,256,256]{2,1,0:T(8,128)(2,1)S(1)} %copy-done.1, f32[3,3,256]{2,1,0:T(4,128)S(1)} %copy-done.3, bf16[256,256]{1,0:T(8,128)(2,1)S(1)} %copy-done.2, f32[1,256]{1,0:T(1,128)S(1)} %bitcast.1, bf16[256,4096]{1,0:T(8,128)(2,1)S(1)} %copy-done), custom_call_target="tpu_custom_call" | custom-call | flops 4000000000 | bytes 3000000 | tf_op jit(solution)/shard_map/hyena_operator/pallas_call | solution.py:370
  116.6 0.7 copy.7
Async XLA Ops:
  0.0 1.6 %copy-start = (bf16[256,4096]{1,0:T(8,128)(2,1)S(1)}, bf16[256,4096]{1,0:T(8,128)(2,1)}, u32[]{:S(2)}) copy-start(bf16[256,4096]{1,0:T(8,128)(2,1)} %w_hbm.1) | copy-start | bytes 6291460
  1.6 1.0 copy-start.1
  2.6 0.9 copy-start.2
  3.5 0.7 copy-start.3
  4.2 0.7 copy-start.4

commit v2 on v1

v2 whole, which is shorter than its diff:
```python
import jax
import jax.numpy as jnp
from jax import lax
from jax.experimental import pallas as pl
from jax.experimental.pallas import tpu as pltpu
from jax.sharding import PartitionSpec as P

MESH = pl.DeviceIdType.MESH
F32 = jnp.float32
BF16 = jnp.bfloat16
SIDE = 256
LANES = 128
PARTS = 4
LAG = 4
STEPS = 7 * PARTS


def remote(src, dst, send_sem, recv_sem, device):
    return pltpu.make_async_remote_copy(
        src_ref=src, dst_ref=dst, send_sem=send_sem, recv_sem=recv_sem,
        device_id=device, device_id_type=MESH,
    )


def kernel(
    feat_hbm, taps_hbm, filt_hbm, bias_hbm, w_hbm, out_ref,
    feat, taps, filt, bias_out, w, cols, halo_out, halo_in, bias_in, gate, kv,
    filt_pre, filt_zr, filt_zs, filt_xy, filt_all, kv_xy, kv_zs, kv_zr,
    mix_zs, mix_zr, mix_ss, mix,
    turn, hpad, ahead, behind, xpad, pairs, sums, folded, ypad, piece, xs_buf, toep, gated_t,
    sib_out, sib_in, own, right_out, right_in, right_far, left_out, left_in, left_far,
    load_sem, halo_sem, bias_sem,
    xy_send, xy_recv, z_send, z_recv, kv_send, kv_recv, back_send, back_recv,
    sib_send, sib_recv, right_send, right_recv, left_send, left_recv,
):
    context = lax.axis_index("context")
    tensor = lax.axis_index("tensor")
    x = lax.div(context, 16)
    y = lax.rem(context, 4)
    z_hi = lax.rem(lax.div(context, 4), 4)
    z_lo = lax.div(tensor, 2)
    core = lax.rem(tensor, 2)
    here = x * 4 + y

    def plane(step):
        to_x = lax.rem(x + step // 4, 4)
        to_y = lax.rem(y + step % 4, 4)
        return to_x * 4 + to_y, (to_x * 16 + z_hi * 4 + to_y, tensor)

    opposite = lax.rem(z_lo + 4, 8) * 2 + core

    def across(target_hi):
        return (x * 16 + target_hi * 4 + y, opposite)

    def along(target_lo):
        return (context, target_lo * 2 + core)

    after = (lax.rem(context + 1, 64), tensor)
    before = (lax.rem(context + 63, 64), tensor)
    sibling = (context, z_lo * 2 + 1 - core)
    right = along(lax.rem(z_lo + 1, 8))
    left = along(lax.rem(z_lo + 7, 8))

    def swap_blocks(src, dst):
        for half in range(2):
            lanes = pl.ds(half * LANES, LANES)
            turn[half] = src[:, lanes].astype(F32)
        for j in range(16):
            for half in range(2):
                block = turn[half, pl.ds(j, 16, stride=16), :]
                dst[pl.ds(16 * j, 16), pl.ds(half * LANES, LANES)] = block.astype(BF16)

    loads = [
        pltpu.make_async_copy(feat_hbm, feat, load_sem.at[0]),
        pltpu.make_async_copy(filt_hbm, filt, load_sem.at[1]),
        pltpu.make_async_copy(w_hbm, w, load_sem.at[2]),
        pltpu.make_async_copy(taps_hbm, taps, load_sem.at[3]),
        pltpu.make_async_copy(bias_hbm, bias_out, load_sem.at[4]),
    ]
    for which in (1, 0, 3, 4, 2):
        loads[which].start()

    barrier = pltpu.get_barrier_semaphore()
    peers = [across(lax.rem(z_hi + step, 4)) for step in (2, 1, 3, 0)]
    peers += [before]
    peers += [along(lax.rem(z_lo + step, 8)) for step in range(1, 8)]
    peers += [plane(step)[1] for step in range(1, 16)]
    peers += [sibling]
    for peer in peers:
        pl.semaphore_signal(barrier, inc=1, device_id=peer, device_id_type=MESH)

    loads[1].wait()
    swap_blocks(filt, filt_pre)
    for which in (0, 3, 4):
        loads[which].wait()

    row = lax.broadcasted_iota(jnp.int32, (16, SIDE), 0)
    pos = lax.broadcasted_iota(jnp.int32, (16, SIDE), 1)
    edge = jnp.zeros((16, SIDE), F32)
    for stream in range(3):
        pick = ((row - 2 * stream == pos - (SIDE - 2)) & (pos >= SIDE - 2)).astype(F32).astype(BF16)
        edge = edge + lax.dot_general(
            pick, feat[stream], (((1,), (1,)), ((), ())), preferred_element_type=F32
        )
    halo_out[...] = edge.astype(BF16)
    cols[...] = jnp.zeros((LANES, SIDE), F32)
    for stream in range(3):
        for tap in range(3):
            cols[pl.ds(3 * stream + tap, 1), :] = taps[stream, pl.ds(tap, 1), :]
    hpad[:, 0:8, :] = jnp.zeros((4, 8, LANES), F32)
    xpad[:, 0:8, :] = jnp.zeros((4, 8, LANES), F32)
    pairs[0:32, :] = jnp.zeros((32, LANES), F32)
    sums[0:32, :] = jnp.zeros((32, LANES), F32)

    pl.semaphore_wait(barrier, len(peers))

    sent = []
    halo_copy = remote(halo_out, halo_in, halo_sem.at[0], halo_sem.at[1], after)
    halo_copy.start()
    bias_copy = remote(bias_out, bias_in, bias_sem.at[0], bias_sem.at[1], across(z_hi))
    bias_copy.start()

    sent.extend([halo_copy, bias_copy])

    def plane_exchange(src, dst, which):
        copies = []
        for step in range(1, 16):
            to, device = plane(step)
            copy = remote(
                src.at[pl.ds(pl.multiple_of(to * 16, 16), 16)],
                dst.at[pl.ds(pl.multiple_of(here * 16, 16), 16)],
                xy_send.at[which, step], xy_recv.at[which, step], device,
            )
            copy.start()
            copies.append(copy)
        mine = pl.ds(pl.multiple_of(here * 16, 16), 16)
        dst[mine, :] = src[mine, :]
        sent.extend(copies)
        return copies

    def across_exchange(src, dst, send, recv, first, rows):
        copies = []
        for step in (2, 1, 3, 0):
            to = lax.rem(z_hi + step, 4)
            copy = remote(
                src.at[pl.ds(pl.multiple_of(to * 64 + first, 16), rows)],
                dst.at[pl.ds(pl.multiple_of(z_hi * 64 + first, 16), rows)],
                send.at[step], recv.at[step], across(to),
            )
            copy.start()
            copies.append(copy)
        sent.extend(copies)
        return copies

    def arrived(copies):
        for copy in copies:
            copy.wait_recv()

    def spread(src, dst, start, ch):
        for zs in range(4):
            tile = src[pl.ds(zs * 64 + ch * 16, 16), :].astype(F32)
            for xs in range(4):
                for half in range(2):
                    first = start + (xs * 16 + zs * 4) * 2 + half
                    dst[ch, pl.ds(first, 4, stride=2), :] = tile[
                        4 * xs : 4 * xs + 4, half * LANES : (half + 1) * LANES
                    ]

    filt_across = across_exchange(filt_pre, filt_zr, z_send, z_recv, 0, 64)

    halo_copy.wait_recv()
    seen = jnp.where(context > 0, 1.0, 0.0)
    cols[16:32, :] = halo_in[...].astype(F32) * seen
    turned = cols[...].T
    lane = lax.broadcasted_iota(jnp.int32, (64, SIDE), 1)
    for block in range(4):
        rows = slice(64 * block, 64 * block + 64)
        shaped = []
        for stream in range(3):
            now = feat[stream, rows, :].astype(F32)
            last = turned[rows, 16 + 2 * stream + 1 : 16 + 2 * stream + 2]
            older = turned[rows, 16 + 2 * stream : 16 + 2 * stream + 1]
            one = jnp.where(lane == 0, last, pltpu.roll(now, 1, 1))
            two = jnp.where(lane == 0, older, jnp.where(lane == 1, last, pltpu.roll(now, 2, 1)))
            tap = [turned[rows, 3 * stream + j : 3 * stream + j + 1] for j in range(3)]
            shaped.append(tap[0] * now + tap[1] * one + tap[2] * two)
        gate[rows, :] = shaped[0].astype(BF16)
        kv[rows, :] = (shaped[1] * shaped[2]).astype(BF16)

    kv_plane = plane_exchange(kv, kv_xy, 1)
    arrived(kv_plane)
    swap_blocks(kv_xy, kv_zs)
    kv_across = [
        across_exchange(kv_zs, kv_zr, kv_send.at[ch], kv_recv.at[ch], 16 * ch, 16)
        for ch in range(4)
    ]

    arrived(filt_across)
    swap_blocks(filt_zr, filt_zs)
    arrived(plane_exchange(filt_zs, filt_xy, 0))
    swap_blocks(filt_xy, filt_all)
    for ch in range(4):
        spread(filt_all, hpad, 8, ch)

    low = lax.broadcasted_iota(jnp.int32, (16, LANES), 1) < 64
    for ch in range(4):
        for a in range(4):
            one = hpad[ch, pl.ds(8 + 32 * a, 16), :]
            two = hpad[ch, pl.ds(24 + 32 * a, 16), :]
            even = jnp.where(low, one, pltpu.roll(two, 64, 1))
            odd = jnp.where(low, pltpu.roll(one, 64, 1), two)
            ahead[ch, pl.ds(32 * a, 16, stride=2), :] = even
            ahead[ch, pl.ds(32 * a + 1, 16, stride=2), :] = odd
            behind[ch, pl.ds(32 * a + 1, 16, stride=2), :] = pltpu.roll(even, 64, 1)
            behind[ch, pl.ds(32 * a + 2, 16, stride=2), :] = pltpu.roll(odd, 64, 1)
        for a in range(4):
            one = hpad[ch, pl.ds(23 + 32 * a, 1), :]
            two = hpad[ch, pl.ds(7 + 32 * a, 1), :]
            behind[ch, pl.ds(32 * a, 1), :] = jnp.where(low[:1], pltpu.roll(one, 64, 1), two)
    lane = lax.broadcasted_iota(jnp.int32, (64, LANES), 1)
    down = lax.broadcasted_iota(jnp.int32, (64, LANES), 0)
    keep = lax.rem(lane, 64) + down < 64

    def build(index, carry):
        ch = lax.div(index, 32)
        b = lax.rem(index, 32)
        for a in range(4):
            block = jnp.where(
                keep,
                jnp.broadcast_to(ahead[ch, pl.ds(32 * a + b, 1), :], (64, LANES)),
                jnp.broadcast_to(behind[ch, pl.ds(32 * a + b, 1), :], (64, LANES)),
            )
            block = pltpu.roll(block, 0, 1, stride=1, stride_axis=0)
            toep[ch, pl.ds(pl.multiple_of(b * 64, 64), 64), pl.ds(a * LANES, LANES)] = (
                block.astype(BF16)
            )
        return carry

    lax.fori_loop(0, 128, build, 0)

    bias_copy.wait_recv()
    spot = lax.broadcasted_iota(jnp.int32, (1, SIDE), 1)
    first_lanes = lax.broadcasted_iota(jnp.int32, (LANES, LANES), 1) < 64
    back = []
    for ch in range(4):
        arrived(kv_across[ch])
        spread(kv_zr, xpad, 8, ch)
        own_row = xpad[ch, pl.ds(8, LANES), :]
        row_before = xpad[ch, pl.ds(7, LANES), :]
        pairs[pl.ds(32, LANES, stride=2), :] = jnp.where(first_lanes, own_row, row_before)
        pairs[pl.ds(33, LANES, stride=2), :] = pltpu.roll(own_row, 64, 1)
        for b in range(16):
            xs_buf[:, pl.ds(b * LANES, LANES)] = pairs[pl.ds(32 - 2 * b, SIDE), :].astype(BF16)
        upper = jnp.dot(xs_buf[...], toep[ch, :, pl.ds(0, SIDE)], preferred_element_type=F32)
        lower = jnp.dot(
            xs_buf[pl.ds(0, LANES), :], toep[ch, :, pl.ds(SIDE, SIDE)],
            preferred_element_type=F32,
        )
        sums[pl.ds(32, SIDE), :] = upper[:, :LANES]
        sums[pl.ds(96, 192), :] += upper[:192, LANES:]
        sums[pl.ds(160, LANES), :] += lower[:, :LANES]
        sums[pl.ds(224, 64), :] += lower[:64, LANES:]
        folded[...] = sums[pl.ds(32, SIDE), :] + pltpu.roll(sums[pl.ds(0, SIDE), :], 64, 1)
        total = jnp.where(
            first_lanes,
            folded[pl.ds(0, LANES, stride=2), :],
            pltpu.roll(folded[pl.ds(1, LANES, stride=2), :], 64, 1),
        )
        channel = here * 16 + z_hi * 4 + ch
        bias = jnp.sum(jnp.where(spot == channel, bias_in[...], 0.0), axis=1, keepdims=True)
        ypad[...] = total + bias * own_row
        for zs in range(4):
            for xs in range(4):
                for half in range(2):
                    first = (xs * 16 + zs * 4) * 2 + half
                    piece[pl.ds(4 * xs, 4), pl.ds(half * LANES, LANES)] = ypad[
                        pl.ds(first, 4, stride=2), :
                    ]
            mix_zs[pl.ds(zs * 64 + ch * 16, 16), :] = piece[...].astype(BF16)
        back += across_exchange(
            mix_zs, mix_zr, back_send.at[ch], back_recv.at[ch], 16 * ch, 16
        )

    arrived(back)
    swap_blocks(mix_zr, mix_ss)
    arrived(plane_exchange(mix_ss, mix, 2))

    gated = (gate[...].astype(F32) * mix[...].astype(F32)).astype(BF16).astype(F32)
    gated_t[...] = gated.T.astype(BF16)
    loads[2].wait()

    def sib_copy(d):
        return remote(sib_out.at[d], sib_in.at[d], sib_send.at[d], sib_recv.at[d], sibling)

    for d in (7, 0, 6, 1, 5, 2, 4, 3):
        theirs = pl.ds(pl.multiple_of((2 * d + 1 - core) * SIDE, SIDE), SIDE)
        mine = pl.ds(pl.multiple_of((2 * d + core) * SIDE, SIDE), SIDE)
        sib_out[d] = jnp.dot(gated_t[...], w[:, theirs], preferred_element_type=F32).astype(BF16)
        sib_copy(d).start()
        own[d] = jnp.dot(gated_t[...], w[:, mine], preferred_element_type=F32)

    size = SIDE // PARTS

    def rows_of(n):
        return pl.ds(pl.multiple_of(lax.rem(n, PARTS) * size, size), size)

    quarter = lax.rem(z_lo, 4)

    def right_copy(n):
        d = 7 - lax.div(n, PARTS)
        return remote(
            right_out.at[d, rows_of(n)], right_in.at[d, rows_of(n)],
            right_send.at[n], right_recv.at[n], right,
        )

    def right_jump(n, d):
        return remote(
            right_out.at[7 - lax.div(n, PARTS), rows_of(n)], right_far.at[rows_of(n)],
            right_send.at[n], right_recv.at[STEPS + lax.rem(n, PARTS)], along(d),
        )

    def left_copy(n):
        d = lax.div(n, PARTS)
        return remote(
            left_out.at[d, rows_of(n)], left_in.at[d, rows_of(n)],
            left_send.at[n], left_recv.at[n], left,
        )

    def left_jump(n, d):
        return remote(
            left_out.at[lax.div(n, PARTS), rows_of(n)], left_far.at[rows_of(n)],
            left_send.at[n], left_recv.at[STEPS + lax.rem(n, PARTS)], along(d),
        )

    def pass_on(n, d, first, jumps, copy, jump, came, going):
        rows = rows_of(n)

        @pl.when(lax.rem(n, PARTS) == 0)
        def _():
            sib_copy(d).wait_recv()

        @pl.when(first)
        def _():
            going[d, rows, :] = (own[d, rows, :] + sib_in[d, rows, :].astype(F32)).astype(BF16)

        @pl.when(jnp.logical_not(first))
        def _():
            copy.wait_recv()
            going[d, rows, :] = (
                own[d, rows, :] + sib_in[d, rows, :].astype(F32) + came[d, rows, :].astype(F32)
            ).astype(BF16)

        @pl.when(jumps)
        def _():
            jump.start()

        @pl.when(jnp.logical_not(jumps))
        def _():
            copy.start()

    def reduce_step(moment, carry):
        n = moment - quarter * LAG

        @pl.when((n >= 0) & (n < (7 - z_lo) * PARTS))
        def _():
            d = 7 - lax.div(n, PARTS)
            pass_on(
                n, d, quarter == 0, (z_lo == 3) & (d > 4),
                right_copy(n), right_jump(n, d), right_in, right_out,
            )

        m = moment - (3 - quarter) * LAG

        @pl.when((m >= 0) & (m < z_lo * PARTS))
        def _():
            d = lax.div(m, PARTS)
            pass_on(
                m, d, quarter == 3, (z_lo == 4) & (d < 3),
                left_copy(m), left_jump(m, d), left_in, left_out,
            )

        return carry

    lax.fori_loop(0, STEPS + 3 * LAG, reduce_step, 0)

    sib_copy(z_lo).wait_recv()
    own[z_lo] = own[z_lo] + sib_in[z_lo].astype(F32)

    @pl.when(z_lo > 0)
    def _():
        for part in range(PARTS):
            right_copy((7 - z_lo) * PARTS + part).wait_recv()
        own[z_lo] = own[z_lo] + right_in[z_lo].astype(F32)

    @pl.when(z_lo < 7)
    def _():
        for part in range(PARTS):
            left_copy(z_lo * PARTS + part).wait_recv()
        own[z_lo] = own[z_lo] + left_in[z_lo].astype(F32)

    @pl.when(z_lo > 4)
    def _():
        for part in range(PARTS):
            right_jump(part, z_lo).wait_recv()
        own[z_lo] = own[z_lo] + right_far[...].astype(F32)

    @pl.when(z_lo < 3)
    def _():
        for part in range(PARTS):
            left_jump(part, z_lo).wait_recv()
        own[z_lo] = own[z_lo] + left_far[...].astype(F32)

    out_ref[...] = own[z_lo].astype(BF16)

    for copy in sent:
        copy.wait_send()
    for d in range(8):
        sib_copy(d).wait_send()

    def close(n, carry):
        @pl.when(n < (7 - z_lo) * PARTS)
        def _():
            right_copy(n).wait_send()

        @pl.when(n < z_lo * PARTS)
        def _():
            left_copy(n).wait_send()

        return carry

    lax.fori_loop(0, STEPS, close, 0)


def local(features, short_taps, long_filter, skip_bias, out_weight):
    vmem = pl.BlockSpec(memory_space=pltpu.VMEM)
    anywhere = pl.BlockSpec(memory_space=pl.ANY)
    square = pltpu.VMEM((SIDE, SIDE), BF16)
    dma = pltpu.SemaphoreType.DMA
    return pl.pallas_call(
        kernel,
        out_shape=jax.ShapeDtypeStruct((SIDE, SIDE), BF16),
        in_specs=[anywhere] * 5,
        out_specs=vmem,
        scratch_shapes=[
            pltpu.VMEM((3, SIDE, SIDE), BF16),
            pltpu.VMEM((3, 3, SIDE), F32),
            square,
            pltpu.VMEM((1, SIDE), F32),
            pltpu.VMEM((SIDE, 16 * SIDE), BF16),
            pltpu.VMEM((LANES, SIDE), F32),
            pltpu.VMEM((16, SIDE), BF16),
            pltpu.VMEM((16, SIDE), BF16),
            pltpu.VMEM((1, SIDE), F32),
            square, square,
            square, square, square, square, square,
            square, square, square,
            square, square, square, square,
            pltpu.VMEM((2, SIDE, LANES), F32),
            pltpu.VMEM((4, 136, LANES), F32),
            pltpu.VMEM((4, LANES, LANES), F32),
            pltpu.VMEM((4, 136, LANES), F32),
            pltpu.VMEM((4, 136, LANES), F32),
            pltpu.VMEM((32 + SIDE, LANES), F32),
            pltpu.VMEM((32 + SIDE, LANES), F32),
            pltpu.VMEM((SIDE, LANES), F32),
            pltpu.VMEM((LANES, LANES), F32),
            pltpu.VMEM((16, SIDE), F32),
            pltpu.VMEM((SIDE, 2048), BF16),
            pltpu.VMEM((4, 2048, 512), BF16),
            square,
            pltpu.VMEM((8, SIDE, SIDE), BF16),
            pltpu.VMEM((8, SIDE, SIDE), BF16),
            pltpu.VMEM((8, SIDE, SIDE), F32),
            pltpu.VMEM((8, SIDE, SIDE), BF16), pltpu.VMEM((8, SIDE, SIDE), BF16), square,
            pltpu.VMEM((8, SIDE, SIDE), BF16), pltpu.VMEM((8, SIDE, SIDE), BF16), square,
            dma((5,)), dma((2,)), dma((2,)),
            dma((3, 16)), dma((3, 16)),
            dma((4,)), dma((4,)),
            dma((4, 4)), dma((4, 4)),
            dma((4, 4)), dma((4, 4)),
            dma((8,)), dma((8,)),
            dma((STEPS,)), dma((STEPS + PARTS,)), dma((STEPS,)), dma((STEPS + PARTS,)),
        ],
        compiler_params=pltpu.CompilerParams(
            collective_id=0, has_side_effects=True, vmem_limit_bytes=60 << 20
        ),
        cost_estimate=pl.CostEstimate(
            flops=4 * 10**9, bytes_accessed=3 * 10**6, transcendentals=0
        ),
        name="hyena_operator",
    )(features, short_taps, long_filter, skip_bias.reshape(1, SIDE), out_weight)


def solution(mesh):
    placed = (
        P(None, "tensor", "context"),
        P(None, None, "tensor"),
        P("tensor", "context"),
        P("tensor"),
        P("tensor", None),
    )
    return jax.shard_map(
        local, mesh=mesh, in_specs=placed, out_specs=P("context", "tensor"), check_vma=False
    )
```

time: 118 us -> 113 us (0.958)
  the two profiles are of different devices: /device:TPU:24 before, /device:TPU:128 now
where the time goes in v2:
time: 113 us
  Pallas kernels  111 us (98%)
  local copies, waits for them, and re-layouts  1.57 us (1%)
    pallas_call x1, Pallas kernels, local(): pl.pallas_call(kernel, out_shape=jax.ShapeDtypeStruct((SIDE, SIDE), BF16)...  111 us

profile of v2, /device:TPU:128, one launch (start us, length us, event | category | flops | bytes accessed | tf_op | source)
XLA Modules:
  0.0 113.0 jit_solution(313661605650942940)
XLA Ops:
  0.0 111.4 %hyena_operator.1 = bf16[256,256]{1,0:T(8,128)(2,1)} custom-call(bf16[3,256,256]{2,1,0:T(8,128)(2,1)} %feat_hbm.1, f32[3,3,256]{2,1,0:T(4,128)} %taps_hbm.1, bf16[256,256]{1,0:T(8,128)(2,1)} %filt_hbm.1, f32[1,256]{1,0:T(1,128)} %bitcast.1, bf16[256,4096]{1,0:T(8,128)(2,1)} %w_hbm.1), custom_call_target="tpu_custom_call" | custom-call | flops 4000000000 | bytes 3000000 | tf_op jit(solution)/shard_map/hyena_operator/pallas_call | solution.py:439
  111.4 1.6 %copy.7 = bf16[256,256]{1,0:T(8,128)(2,1)} copy(bf16[256,256]{1,0:T(8,128)(2,1)} %hyena_operator.1) | data formatting | bytes 262144

commit v3 on v2

--- a/solution.py
+++ b/solution.py
@@ -10,7 +10,7 @@
 BF16 = jnp.bfloat16
 SIDE = 256
 LANES = 128
-PARTS = 4
+PARTS = 2
 LAG = 4
 STEPS = 7 * PARTS
 
@@ -241,7 +241,14 @@
     bias_copy.wait_recv()
     spot = lax.broadcasted_iota(jnp.int32, (1, SIDE), 1)
     first_lanes = lax.broadcasted_iota(jnp.int32, (LANES, LANES), 1) < 64
-    back = []
+    back = ([], [])
+
+    def send_back(half, ch):
+        back[half].extend(across_exchange(
+            mix_zs.at[half], mix_zr.at[half], back_send.at[half, ch], back_recv.at[half, ch],
+            16 * ch, 16,
+        ))
+
     for ch in range(4):
         arrived(kv_across[ch])
         spread(kv_zr, xpad, 8, ch)
@@ -270,74 +277,88 @@
         bias = jnp.sum(jnp.where(spot == channel, bias_in[...], 0.0), axis=1, keepdims=True)
         ypad[...] = total + bias * own_row
         for zs in range(4):
-            for xs in range(4):
-                for half in range(2):
-                    first = (xs * 16 + zs * 4) * 2 + half
-                    piece[pl.ds(4 * xs, 4), pl.ds(half * LANES, LANES)] = ypad[
-                        pl.ds(first, 4, stride=2), :
+            for half in range(2):
+                for xs in range(4):
+                    piece[pl.ds(4 * xs, 4), :] = ypad[
+                        pl.ds((xs * 16 + zs * 4) * 2 + half, 4, stride=2), :
                     ]
-            mix_zs[pl.ds(zs * 64 + ch * 16, 16), :] = piece[...].astype(BF16)
-        back += across_exchange(
-            mix_zs, mix_zr, back_send.at[ch], back_recv.at[ch], 16 * ch, 16
-        )
-
-    arrived(back)
-    swap_blocks(mix_zr, mix_ss)
-    arrived(plane_exchange(mix_ss, mix, 2))
-
-    gated = (gate[...].astype(F32) * mix[...].astype(F32)).astype(BF16).astype(F32)
-    gated_t[...] = gated.T.astype(BF16)
-    loads[2].wait()
-
-    def sib_copy(d):
-        return remote(sib_out.at[d], sib_in.at[d], sib_send.at[d], sib_recv.at[d], sibling)
-
-    for d in (7, 0, 6, 1, 5, 2, 4, 3):
-        theirs = pl.ds(pl.multiple_of((2 * d + 1 - core) * SIDE, SIDE), SIDE)
-        mine = pl.ds(pl.multiple_of((2 * d + core) * SIDE, SIDE), SIDE)
-        sib_out[d] = jnp.dot(gated_t[...], w[:, theirs], preferred_element_type=F32).astype(BF16)
-        sib_copy(d).start()
-        own[d] = jnp.dot(gated_t[...], w[:, mine], preferred_element_type=F32)
-
-    size = SIDE // PARTS
-
-    def rows_of(n):
-        return pl.ds(pl.multiple_of(lax.rem(n, PARTS) * size, size), size)
+                mix_zs[half, pl.ds(zs * 64 + ch * 16, 16), :] = piece[...].astype(BF16)
+        send_back(0, ch)
+        if ch < 2:
+            send_back(1, ch)
+    send_back(1, 2)
+    send_back(1, 3)
+
+    def sib_copy(half, d):
+        rows = pl.ds(half * LANES, LANES)
+        return remote(
+            sib_out.at[d, rows], sib_in.at[d, rows],
+            sib_send.at[half, d], sib_recv.at[half, d], sibling,
+        )
+
+    def swap_half(half):
+        turn[half] = mix_zr[half].astype(F32)
+        for j in range(16):
+            mix_ss[half, pl.ds(16 * j, 16), :] = turn[half, pl.ds(j, 16, stride=16), :].astype(BF16)
+
+    def to_plane(half):
+        arrived(back[half])
+        swap_half(half)
+        return plane_exchange(mix_ss.at[half], mix.at[half], 2 + half)
+
+    def project(half):
+        lanes = pl.ds(half * LANES, LANES)
+        rows = pl.ds(half * LANES, LANES)
+        gated = gate[:, lanes].astype(F32) * mix[half].astype(F32)
+        gated_t[rows, :] = gated.astype(BF16).astype(F32).T.astype(BF16)
+        for d in (7, 0, 6, 1, 5, 2, 4, 3):
+            theirs = pl.ds(pl.multiple_of((2 * d + 1 - core) * SIDE, SIDE), SIDE)
+            mine = pl.ds(pl.multiple_of((2 * d + core) * SIDE, SIDE), SIDE)
+            sib_out[d, rows, :] = jnp.dot(
+                gated_t[rows, :], w[:, theirs], preferred_element_type=F32
+            ).astype(BF16)
+            sib_copy(half, d).start()
+            own[d, rows, :] = jnp.dot(gated_t[rows, :], w[:, mine], preferred_element_type=F32)
+
+    size = LANES // PARTS
+
+    def rows_of(half, n):
+        return pl.ds(pl.multiple_of(half * LANES + lax.rem(n, PARTS) * size, size), size)
 
     quarter = lax.rem(z_lo, 4)
 
-    def right_copy(n):
+    def right_copy(half, n):
         d = 7 - lax.div(n, PARTS)
         return remote(
-            right_out.at[d, rows_of(n)], right_in.at[d, rows_of(n)],
-            right_send.at[n], right_recv.at[n], right,
-        )
-
-    def right_jump(n, d):
+            right_out.at[d, rows_of(half, n)], right_in.at[d, rows_of(half, n)],
+            right_send.at[half, n], right_recv.at[half, n], right,
+        )
+
+    def right_jump(half, n, d):
         return remote(
-            right_out.at[7 - lax.div(n, PARTS), rows_of(n)], right_far.at[rows_of(n)],
-            right_send.at[n], right_recv.at[STEPS + lax.rem(n, PARTS)], along(d),
-        )
-
-    def left_copy(n):
+            right_out.at[7 - lax.div(n, PARTS), rows_of(half, n)], right_far.at[rows_of(half, n)],
+            right_send.at[half, n], right_recv.at[half, STEPS + lax.rem(n, PARTS)], along(d),
+        )
+
+    def left_copy(half, n):
         d = lax.div(n, PARTS)
         return remote(
-            left_out.at[d, rows_of(n)], left_in.at[d, rows_of(n)],
-            left_send.at[n], left_recv.at[n], left,
-        )
-
-    def left_jump(n, d):
+            left_out.at[d, rows_of(half, n)], left_in.at[d, rows_of(half, n)],
+            left_send.at[half, n], left_recv.at[half, n], left,
+        )
+
+    def left_jump(half, n, d):
         return remote(
-            left_out.at[lax.div(n, PARTS), rows_of(n)], left_far.at[rows_of(n)],
-            left_send.at[n], left_recv.at[STEPS + lax.rem(n, PARTS)], along(d),
-        )
-
-    def pass_on(n, d, first, jumps, copy, jump, came, going):
-        rows = rows_of(n)
+            left_out.at[lax.div(n, PARTS), rows_of(half, n)], left_far.at[rows_of(half, n)],
+            left_send.at[half, n], left_recv.at[half, STEPS + lax.rem(n, PARTS)], along(d),
+        )
+
+    def pass_on(half, n, d, first, jumps, copy, jump, came, going):
+        rows = rows_of(half, n)
 
         @pl.when(lax.rem(n, PARTS) == 0)
         def _():
-            sib_copy(d).wait_recv()
+            sib_copy(half, d).wait_recv()
 
         @pl.when(first)
         def _():
@@ -358,83 +379,98 @@
         def _():
             copy.start()
 
-    def reduce_step(moment, carry):
-        n = moment - quarter * LAG
-
-        @pl.when((n >= 0) & (n < (7 - z_lo) * PARTS))
-        def _():
-            d = 7 - lax.div(n, PARTS)
-            pass_on(
-                n, d, quarter == 0, (z_lo == 3) & (d > 4),
-                right_copy(n), right_jump(n, d), right_in, right_out,
-            )
-
-        m = moment - (3 - quarter) * LAG
-
-        @pl.when((m >= 0) & (m < z_lo * PARTS))
-        def _():
-            d = lax.div(m, PARTS)
-            pass_on(
-                m, d, quarter == 3, (z_lo == 4) & (d < 3),
-                left_copy(m), left_jump(m, d), left_in, left_out,
-            )
-
-        return carry
-
-    lax.fori_loop(0, STEPS + 3 * LAG, reduce_step, 0)
-
-    sib_copy(z_lo).wait_recv()
-    own[z_lo] = own[z_lo] + sib_in[z_lo].astype(F32)
-
-    @pl.when(z_lo > 0)
-    def _():
-        for part in range(PARTS):
-            right_copy((7 - z_lo) * PARTS + part).wait_recv()
-        own[z_lo] = own[z_lo] + right_in[z_lo].astype(F32)
-
-    @pl.when(z_lo < 7)
-    def _():
-        for part in range(PARTS):
-            left_copy(z_lo * PARTS + part).wait_recv()
-        own[z_lo] = own[z_lo] + left_in[z_lo].astype(F32)
-
-    @pl.when(z_lo > 4)
-    def _():
-        for part in range(PARTS):
-            right_jump(part, z_lo).wait_recv()
-        own[z_lo] = own[z_lo] + right_far[...].astype(F32)
-
-    @pl.when(z_lo < 3)
-    def _():
-        for part in range(PARTS):
-            left_jump(part, z_lo).wait_recv()
-        own[z_lo] = own[z_lo] + left_far[...].astype(F32)
+    def reduce_half(half):
+        def reduce_step(moment, carry):
+            n = moment - quarter * LAG
+
+            @pl.when((n >= 0) & (n < (7 - z_lo) * PARTS))
+            def _():
+                d = 7 - lax.div(n, PARTS)
+                pass_on(
+                    half, n, d, quarter == 0, (z_lo == 3) & (d > 4),
+                    right_copy(half, n), right_jump(half, n, d), right_in, right_out,
+                )
+
+            m = moment - (3 - quarter) * LAG
+
+            @pl.when((m >= 0) & (m < z_lo * PARTS))
+            def _():
+                d = lax.div(m, PARTS)
+                pass_on(
+                    half, m, d, quarter == 3, (z_lo == 4) & (d < 3),
+                    left_copy(half, m), left_jump(half, m, d), left_in, left_out,
+                )
+
+            return carry
+
+        lax.fori_loop(0, STEPS + 3 * LAG, reduce_step, 0)
+
+    first_plane = to_plane(0)
+    arrived(first_plane)
+    loads[2].wait()
+    project(0)
+    second_plane = to_plane(1)
+    reduce_half(0)
+    arrived(second_plane)
+    project(1)
+    reduce_half(1)
+
+    for half in range(2):
+        rows = pl.ds(half * LANES, LANES)
+        sib_copy(half, z_lo).wait_recv()
+        own[z_lo, rows, :] += sib_in[z_lo, rows, :].astype(F32)
+
+        @pl.when(z_lo > 0)
+        def _():
+            for part in range(PARTS):
+                right_copy(half, (7 - z_lo) * PARTS + part).wait_recv()
+            own[z_lo, rows, :] += right_in[z_lo, rows, :].astype(F32)
+
+        @pl.when(z_lo < 7)
+        def _():
+            for part in range(PARTS):
+                left_copy(half, z_lo * PARTS + part).wait_recv()
+            own[z_lo, rows, :] += left_in[z_lo, rows, :].astype(F32)
+
+        @pl.when(z_lo > 4)
+        def _():
+            for part in range(PARTS):
+                right_jump(half, part, z_lo).wait_recv()
+            own[z_lo, rows, :] += right_far[rows, :].astype(F32)
+
+        @pl.when(z_lo < 3)
+        def _():
+            for part in range(PARTS):
+                left_jump(half, part, z_lo).wait_recv()
+            own[z_lo, rows, :] += left_far[rows, :].astype(F32)
 
     out_ref[...] = own[z_lo].astype(BF16)
 
     for copy in sent:
         copy.wait_send()
-    for d in range(8):
-        sib_copy(d).wait_send()
-
-    def close(n, carry):
-        @pl.when(n < (7 - z_lo) * PARTS)
-        def _():
-            right_copy(n).wait_send()
-
-        @pl.when(n < z_lo * PARTS)
-        def _():
-            left_copy(n).wait_send()
-
-        return carry
-
-    lax.fori_loop(0, STEPS, close, 0)
+    for half in range(2):
+        for d in range(8):
+            sib_copy(half, d).wait_send()
+
+        def close(n, carry):
+            @pl.when(n < (7 - z_lo) * PARTS)
+            def _():
+                right_copy(half, n).wait_send()
+
+            @pl.when(n < z_lo * PARTS)
+            def _():
+                left_copy(half, n).wait_send()
+
+            return carry
+
+        lax.fori_loop(0, STEPS, close, 0)
 
 
 def local(features, short_taps, long_filter, skip_bias, out_weight):
     vmem = pl.BlockSpec(memory_space=pltpu.VMEM)
     anywhere = pl.BlockSpec(memory_space=pl.ANY)
     square = pltpu.VMEM((SIDE, SIDE), BF16)
+    halves = pltpu.VMEM((2, SIDE, LANES), BF16)
     dma = pltpu.SemaphoreType.DMA
     return pl.pallas_call(
         kernel,
@@ -454,7 +490,7 @@
             square, square,
             square, square, square, square, square,
             square, square, square,
-            square, square, square, square,
+            halves, halves, halves, halves,
             pltpu.VMEM((2, SIDE, LANES), F32),
             pltpu.VMEM((4, 136, LANES), F32),
             pltpu.VMEM((4, LANES, LANES), F32),
@@ -464,7 +500,7 @@
             pltpu.VMEM((32 + SIDE, LANES), F32),
             pltpu.VMEM((SIDE, LANES), F32),
             pltpu.VMEM((LANES, LANES), F32),
-            pltpu.VMEM((16, SIDE), F32),
+            pltpu.VMEM((16, LANES), F32),
             pltpu.VMEM((SIDE, 2048), BF16),
             pltpu.VMEM((4, 2048, 512), BF16),
             square,
@@ -474,12 +510,13 @@
             pltpu.VMEM((8, SIDE, SIDE), BF16), pltpu.VMEM((8, SIDE, SIDE), BF16), square,
             pltpu.VMEM((8, SIDE, SIDE), BF16), pltpu.VMEM((8, SIDE, SIDE), BF16), square,
             dma((5,)), dma((2,)), dma((2,)),
-            dma((3, 16)), dma((3, 16)),
+            dma((4, 16)), dma((4, 16)),
             dma((4,)), dma((4,)),
             dma((4, 4)), dma((4, 4)),
-            dma((4, 4)), dma((4, 4)),
-            dma((8,)), dma((8,)),
-            dma((STEPS,)), dma((STEPS + PARTS,)), dma((STEPS,)), dma((STEPS + PARTS,)),
+            dma((2, 4, 4)), dma((2, 4, 4)),
+            dma((2, 8)), dma((2, 8)),
+            dma((2, STEPS)), dma((2, STEPS + PARTS)),
+            dma((2, STEPS)), dma((2, STEPS + PARTS)),
         ],
         compiler_params=pltpu.CompilerParams(
             collective_id=0, has_side_effects=True, vmem_limit_bytes=60 << 20

time: 113 us -> 123 us (1.088)
  the two profiles are of different devices: /device:TPU:128 before, /device:TPU:64 now
where the time goes in v3:
time: 123 us
  Pallas kernels  122 us (99%)
  local copies, waits for them, and re-layouts  1.57 us (1%)
    pallas_call x1, Pallas kernels, local(): pl.pallas_call(kernel, out_shape=jax.ShapeDtypeStruct((SIDE, SIDE), BF16)...  122 us

profile of v3, /device:TPU:64, one launch (start us, length us, event | category | flops | bytes accessed | tf_op | source)
XLA Modules:
  0.0 123.3 jit_solution(1116109731239467635)
XLA Ops:
  0.0 121.7 %hyena_operator.1 = bf16[256,256]{1,0:T(8,128)(2,1)} custom-call(bf16[3,256,256]{2,1,0:T(8,128)(2,1)} %feat_hbm.1, f32[3,3,256]{2,1,0:T(4,128)} %taps_hbm.1, bf16[256,256]{1,0:T(8,128)(2,1)} %filt_hbm.1, f32[1,256]{1,0:T(1,128)} %bitcast.1, bf16[256,4096]{1,0:T(8,128)(2,1)} %w_hbm.1), custom_call_target="tpu_custom_call" | custom-call | flops 4000000000 | bytes 3000000 | tf_op jit(solution)/shard_map/hyena_operator/pallas_call | solution.py:475
  121.7 1.6 %copy.7 = bf16[256,256]{1,0:T(8,128)(2,1)} copy(bf16[256,256]{1,0:T(8,128)(2,1)} %hyena_operator.1) | data formatting | bytes 262144

commit v4 on v3

--- a/solution.py
+++ b/solution.py
@@ -379,41 +379,42 @@
         def _():
             copy.start()
 
-    def reduce_half(half):
-        def reduce_step(moment, carry):
-            n = moment - quarter * LAG
-
-            @pl.when((n >= 0) & (n < (7 - z_lo) * PARTS))
-            def _():
-                d = 7 - lax.div(n, PARTS)
-                pass_on(
-                    half, n, d, quarter == 0, (z_lo == 3) & (d > 4),
-                    right_copy(half, n), right_jump(half, n, d), right_in, right_out,
-                )
-
-            m = moment - (3 - quarter) * LAG
-
-            @pl.when((m >= 0) & (m < z_lo * PARTS))
-            def _():
-                d = lax.div(m, PARTS)
-                pass_on(
-                    half, m, d, quarter == 3, (z_lo == 4) & (d < 3),
-                    left_copy(half, m), left_jump(half, m, d), left_in, left_out,
-                )
-
-            return carry
-
-        lax.fori_loop(0, STEPS + 3 * LAG, reduce_step, 0)
+    def reduce_step(moment, carry):
+        n = moment - quarter * LAG
+        n_half = jnp.where(n < STEPS, 0, 1)
+        n_here = n - n_half * STEPS
+
+        @pl.when((n >= 0) & (n_here < (7 - z_lo) * PARTS))
+        def _():
+            d = 7 - lax.div(n_here, PARTS)
+            pass_on(
+                n_half, n_here, d, quarter == 0, (z_lo == 3) & (d > 4),
+                right_copy(n_half, n_here), right_jump(n_half, n_here, d), right_in, right_out,
+            )
+
+        m = moment - (3 - quarter) * LAG
+        m_half = jnp.where(m < STEPS, 0, 1)
+        m_here = m - m_half * STEPS
+
+        @pl.when((m >= 0) & (m_here < z_lo * PARTS))
+        def _():
+            d = lax.div(m_here, PARTS)
+            pass_on(
+                m_half, m_here, d, quarter == 3, (z_lo == 4) & (d < 3),
+                left_copy(m_half, m_here), left_jump(m_half, m_here, d), left_in, left_out,
+            )
+
+        return carry
 
     first_plane = to_plane(0)
     arrived(first_plane)
     loads[2].wait()
     project(0)
     second_plane = to_plane(1)
-    reduce_half(0)
+    lax.fori_loop(0, STEPS, reduce_step, 0)
     arrived(second_plane)
     project(1)
-    reduce_half(1)
+    lax.fori_loop(STEPS, 2 * STEPS + 3 * LAG, reduce_step, 0)
 
     for half in range(2):
         rows = pl.ds(half * LANES, LANES)

time: 123 us -> 122 us (level)
  the two profiles are of different devices: /device:TPU:64 before, /device:TPU:24 now
where the time goes in v4:
time: 122 us; the launch traced here: 120 us
  Pallas kernels  118 us (97%)
  local copies, waits for them, and re-layouts  1.57 us (1%)
    pallas_call x1, Pallas kernels, local(): pl.pallas_call(kernel, out_shape=jax.ShapeDtypeStruct((SIDE, SIDE), BF16)...  118 us

profile of v4, /device:TPU:24, one launch (start us, length us, event | category | flops | bytes accessed | tf_op | source)
XLA Modules:
  0.0 120.0 jit_solution(8218420023169382471)
XLA Ops:
  0.0 118.5 %hyena_operator.1 = bf16[256,256]{1,0:T(8,128)(2,1)} custom-call(bf16[3,256,256]{2,1,0:T(8,128)(2,1)} %feat_hbm.1, f32[3,3,256]{2,1,0:T(4,128)} %taps_hbm.1, bf16[256,256]{1,0:T(8,128)(2,1)} %filt_hbm.1, f32[1,256]{1,0:T(1,128)} %bitcast.1, bf16[256,4096]{1,0:T(8,128)(2,1)} %w_hbm.1), custom_call_target="tpu_custom_call" | custom-call | flops 4000000000 | bytes 3000000 | tf_op jit(solution)/shard_map/hyena_operator/pallas_call | solution.py:476
  118.5 1.6 %copy.7 = bf16[256,256]{1,0:T(8,128)(2,1)} copy(bf16[256,256]{1,0:T(8,128)(2,1)} %hyena_operator.1) | data formatting | bytes 262144

commit v5 on v2

--- a/solution.py
+++ b/solution.py
@@ -70,6 +70,11 @@
                 block = turn[half, pl.ds(j, 16, stride=16), :]
                 dst[pl.ds(16 * j, 16), pl.ds(half * LANES, LANES)] = block.astype(BF16)
 
+    def swap_half(src, dst, half):
+        turn[half] = src[half].astype(F32)
+        for j in range(16):
+            dst[half, pl.ds(16 * j, 16), :] = turn[half, pl.ds(j, 16, stride=16), :].astype(BF16)
+
     loads = [
         pltpu.make_async_copy(feat_hbm, feat, load_sem.at[0]),
         pltpu.make_async_copy(filt_hbm, filt, load_sem.at[1]),
@@ -112,6 +117,32 @@
     pairs[0:32, :] = jnp.zeros((32, LANES), F32)
     sums[0:32, :] = jnp.zeros((32, LANES), F32)
 
+    lane = lax.broadcasted_iota(jnp.int32, (64, SIDE), 1)
+
+    def shape(half, halo):
+        turned = cols[...].T
+        part = slice(half * LANES, (half + 1) * LANES)
+        for block in range(4):
+            rows = slice(64 * block, 64 * block + 64)
+            shaped = []
+            for stream in range(3):
+                now = feat[stream, rows, :].astype(F32)
+                one = pltpu.roll(now, 1, 1)
+                two = pltpu.roll(now, 2, 1)
+                if halo:
+                    last = turned[rows, 16 + 2 * stream + 1 : 16 + 2 * stream + 2]
+                    older = turned[rows, 16 + 2 * stream : 16 + 2 * stream + 1]
+                    one = jnp.where(lane == 0, last, one)
+                    two = jnp.where(lane == 0, older, jnp.where(lane == 1, last, two))
+                tap = [turned[rows, 3 * stream + j : 3 * stream + j + 1] for j in range(3)]
+                shaped.append(
+                    tap[0] * now[:, part] + tap[1] * one[:, part] + tap[2] * two[:, part]
+                )
+            gate[rows, part] = shaped[0].astype(BF16)
+            kv[half, rows, :] = (shaped[1] * shaped[2]).astype(BF16)
+
+    shape(1, False)
+
     pl.semaphore_wait(barrier, len(peers))
 
     sent = []
@@ -156,51 +187,40 @@
         for copy in copies:
             copy.wait_recv()
 
-    def spread(src, dst, start, ch):
+    def spread(tile_of, dst, start, ch):
         for zs in range(4):
-            tile = src[pl.ds(zs * 64 + ch * 16, 16), :].astype(F32)
-            for xs in range(4):
-                for half in range(2):
+            for half in range(2):
+                tile = tile_of(half, pl.ds(zs * 64 + ch * 16, 16)).astype(F32)
+                for xs in range(4):
                     first = start + (xs * 16 + zs * 4) * 2 + half
-                    dst[ch, pl.ds(first, 4, stride=2), :] = tile[
-                        4 * xs : 4 * xs + 4, half * LANES : (half + 1) * LANES
-                    ]
+                    dst[ch, pl.ds(first, 4, stride=2), :] = tile[4 * xs : 4 * xs + 4, :]
 
     filt_across = across_exchange(filt_pre, filt_zr, z_send, z_recv, 0, 64)
+
+    kv_plane = plane_exchange(kv.at[1], kv_xy.at[1], 1)
+    arrived(kv_plane)
+    swap_half(kv_xy, kv_zs, 1)
+    kv_across = across_exchange(
+        kv_zs.at[1], kv_zr.at[1], kv_send.at[1], kv_recv.at[1], 0, 64
+    )
 
     halo_copy.wait_recv()
     seen = jnp.where(context > 0, 1.0, 0.0)
     cols[16:32, :] = halo_in[...].astype(F32) * seen
-    turned = cols[...].T
-    lane = lax.broadcasted_iota(jnp.int32, (64, SIDE), 1)
-    for block in range(4):
-        rows = slice(64 * block, 64 * block + 64)
-        shaped = []
-        for stream in range(3):
-            now = feat[stream, rows, :].astype(F32)
-            last = turned[rows, 16 + 2 * stream + 1 : 16 + 2 * stream + 2]
-            older = turned[rows, 16 + 2 * stream : 16 + 2 * stream + 1]
-            one = jnp.where(lane == 0, last, pltpu.roll(now, 1, 1))
-            two = jnp.where(lane == 0, older, jnp.where(lane == 1, last, pltpu.roll(now, 2, 1)))
-            tap = [turned[rows, 3 * stream + j : 3 * stream + j + 1] for j in range(3)]
-            shaped.append(tap[0] * now + tap[1] * one + tap[2] * two)
-        gate[rows, :] = shaped[0].astype(BF16)
-        kv[rows, :] = (shaped[1] * shaped[2]).astype(BF16)
-
-    kv_plane = plane_exchange(kv, kv_xy, 1)
+    shape(0, True)
+    kv_plane = plane_exchange(kv.at[0], kv_xy.at[0], 3)
     arrived(kv_plane)
-    swap_blocks(kv_xy, kv_zs)
-    kv_across = [
-        across_exchange(kv_zs, kv_zr, kv_send.at[ch], kv_recv.at[ch], 16 * ch, 16)
-        for ch in range(4)
-    ]
+    swap_half(kv_xy, kv_zs, 0)
+    kv_across += across_exchange(
+        kv_zs.at[0], kv_zr.at[0], kv_send.at[0], kv_recv.at[0], 0, 64
+    )
 
     arrived(filt_across)
     swap_blocks(filt_zr, filt_zs)
     arrived(plane_exchange(filt_zs, filt_xy, 0))
     swap_blocks(filt_xy, filt_all)
     for ch in range(4):
-        spread(filt_all, hpad, 8, ch)
+        spread(lambda half, rows: filt_all[rows, pl.ds(half * LANES, LANES)], hpad, 8, ch)
 
     low = lax.broadcasted_iota(jnp.int32, (16, LANES), 1) < 64
     for ch in range(4):
@@ -241,10 +261,10 @@
     bias_copy.wait_recv()
     spot = lax.broadcasted_iota(jnp.int32, (1, SIDE), 1)
     first_lanes = lax.broadcasted_iota(jnp.int32, (LANES, LANES), 1) < 64
+    arrived(kv_across)
     back = []
     for ch in range(4):
-        arrived(kv_across[ch])
-        spread(kv_zr, xpad, 8, ch)
+        spread(lambda half, rows: kv_zr[half, rows, :], xpad, 8, ch)
         own_row = xpad[ch, pl.ds(8, LANES), :]
         row_before = xpad[ch, pl.ds(7, LANES), :]
         pairs[pl.ds(32, LANES, stride=2), :] = jnp.where(first_lanes, own_row, row_before)
@@ -277,9 +297,11 @@
                         pl.ds(first, 4, stride=2), :
                     ]
             mix_zs[pl.ds(zs * 64 + ch * 16, 16), :] = piece[...].astype(BF16)
-        back += across_exchange(
-            mix_zs, mix_zr, back_send.at[ch], back_recv.at[ch], 16 * ch, 16
-        )
+        if ch % 2:
+            group = ch // 2
+            back += across_exchange(
+                mix_zs, mix_zr, back_send.at[group], back_recv.at[group], 32 * group, 32
+            )
 
     arrived(back)
     swap_blocks(mix_zr, mix_ss)
@@ -435,6 +457,7 @@
     vmem = pl.BlockSpec(memory_space=pltpu.VMEM)
     anywhere = pl.BlockSpec(memory_space=pl.ANY)
     square = pltpu.VMEM((SIDE, SIDE), BF16)
+    halves = pltpu.VMEM((2, SIDE, LANES), BF16)
     dma = pltpu.SemaphoreType.DMA
     return pl.pallas_call(
         kernel,
@@ -451,9 +474,9 @@
             pltpu.VMEM((16, SIDE), BF16),
             pltpu.VMEM((16, SIDE), BF16),
             pltpu.VMEM((1, SIDE), F32),
-            square, square,
+            square, halves,
             square, square, square, square, square,
-            square, square, square,
+            halves, halves, halves,
             square, square, square, square,
             pltpu.VMEM((2, SIDE, LANES), F32),
             pltpu.VMEM((4, 136, LANES), F32),
@@ -474,10 +497,10 @@
             pltpu.VMEM((8, SIDE, SIDE), BF16), pltpu.VMEM((8, SIDE, SIDE), BF16), square,
             pltpu.VMEM((8, SIDE, SIDE), BF16), pltpu.VMEM((8, SIDE, SIDE), BF16), square,
             dma((5,)), dma((2,)), dma((2,)),
-            dma((3, 16)), dma((3, 16)),
+            dma((4, 16)), dma((4, 16)),
             dma((4,)), dma((4,)),
-            dma((4, 4)), dma((4, 4)),
-            dma((4, 4)), dma((4, 4)),
+            dma((2, 4)), dma((2, 4)),
+            dma((2, 4)), dma((2, 4)),
             dma((8,)), dma((8,)),
             dma((STEPS,)), dma((STEPS + PARTS,)), dma((STEPS,)), dma((STEPS + PARTS,)),
         ],

time: 113 us -> 114 us (level)
  the two profiles are of different devices: /device:TPU:128 before, /device:TPU:96 now
where the time goes in v5:
time: 114 us
  Pallas kernels  113 us (99%)
  local copies, waits for them, and re-layouts  1.57 us (1%)
    pallas_call x1, Pallas kernels, local(): pl.pallas_call(kernel, out_shape=jax.ShapeDtypeStruct((SIDE, SIDE), BF16)...  113 us

profile of v5, /device:TPU:96, one launch (start us, length us, event | category | flops | bytes accessed | tf_op | source)
XLA Modules:
  0.0 114.3 jit_solution(7370334880794926141)
XLA Ops:
  0.0 112.7 %hyena_operator.1 = bf16[256,256]{1,0:T(8,128)(2,1)} custom-call(bf16[3,256,256]{2,1,0:T(8,128)(2,1)} %feat_hbm.1, f32[3,3,256]{2,1,0:T(4,128)} %taps_hbm.1, bf16[256,256]{1,0:T(8,128)(2,1)} %filt_hbm.1, f32[1,256]{1,0:T(1,128)} %bitcast.1, bf16[256,4096]{1,0:T(8,128)(2,1)} %w_hbm.1), custom_call_target="tpu_custom_call" | custom-call | flops 4000000000 | bytes 3000000 | tf_op jit(solution)/shard_map/hyena_operator/pallas_call | solution.py:462
  112.8 1.6 %copy.7 = bf16[256,256]{1,0:T(8,128)(2,1)} copy(bf16[256,256]{1,0:T(8,128)(2,1)} %hyena_operator.1) | data formatting | bytes 262144

commit v6 on v2

--- a/solution.py
+++ b/solution.py
@@ -13,6 +13,7 @@
 PARTS = 4
 LAG = 4
 STEPS = 7 * PARTS
+PLACES = (10, 9, 11, 6, 14, 2, 8, 5, 7, 13, 15, 1, 3, 4, 12)
 
 
 def remote(src, dst, send_sem, recv_sem, device):
@@ -84,7 +85,7 @@
     peers = [across(lax.rem(z_hi + step, 4)) for step in (2, 1, 3, 0)]
     peers += [before]
     peers += [along(lax.rem(z_lo + step, 8)) for step in range(1, 8)]
-    peers += [plane(step)[1] for step in range(1, 16)]
+    peers += [plane(step)[1] for step in PLACES]
     peers += [sibling]
     for peer in peers:
         pl.semaphore_signal(barrier, inc=1, device_id=peer, device_id_type=MESH)
@@ -112,6 +113,32 @@
     pairs[0:32, :] = jnp.zeros((32, LANES), F32)
     sums[0:32, :] = jnp.zeros((32, LANES), F32)
 
+    lane = lax.broadcasted_iota(jnp.int32, (64, SIDE), 1)
+
+    def shape(half, halo):
+        turned = cols[...].T
+        part = slice(half * LANES, (half + 1) * LANES)
+        for block in range(4):
+            rows = slice(64 * block, 64 * block + 64)
+            shaped = []
+            for stream in range(3):
+                now = feat[stream, rows, :].astype(F32)
+                one = pltpu.roll(now, 1, 1)
+                two = pltpu.roll(now, 2, 1)
+                if halo:
+                    last = turned[rows, 16 + 2 * stream + 1 : 16 + 2 * stream + 2]
+                    older = turned[rows, 16 + 2 * stream : 16 + 2 * stream + 1]
+                    one = jnp.where(lane == 0, last, one)
+                    two = jnp.where(lane == 0, older, jnp.where(lane == 1, last, two))
+                tap = [turned[rows, 3 * stream + j : 3 * stream + j + 1] for j in range(3)]
+                shaped.append(
+                    tap[0] * now[:, part] + tap[1] * one[:, part] + tap[2] * two[:, part]
+                )
+            gate[rows, part] = shaped[0].astype(BF16)
+            kv[rows, part] = (shaped[1] * shaped[2]).astype(BF16)
+
+    shape(1, False)
+
     pl.semaphore_wait(barrier, len(peers))
 
     sent = []
@@ -124,7 +151,7 @@
 
     def plane_exchange(src, dst, which):
         copies = []
-        for step in range(1, 16):
+        for step in PLACES:
             to, device = plane(step)
             copy = remote(
                 src.at[pl.ds(pl.multiple_of(to * 16, 16), 16)],
@@ -171,21 +198,7 @@
     halo_copy.wait_recv()
     seen = jnp.where(context > 0, 1.0, 0.0)
     cols[16:32, :] = halo_in[...].astype(F32) * seen
-    turned = cols[...].T
-    lane = lax.broadcasted_iota(jnp.int32, (64, SIDE), 1)
-    for block in range(4):
-        rows = slice(64 * block, 64 * block + 64)
-        shaped = []
-        for stream in range(3):
-            now = feat[stream, rows, :].astype(F32)
-            last = turned[rows, 16 + 2 * stream + 1 : 16 + 2 * stream + 2]
-            older = turned[rows, 16 + 2 * stream : 16 + 2 * stream + 1]
-            one = jnp.where(lane == 0, last, pltpu.roll(now, 1, 1))
-            two = jnp.where(lane == 0, older, jnp.where(lane == 1, last, pltpu.roll(now, 2, 1)))
-            tap = [turned[rows, 3 * stream + j : 3 * stream + j + 1] for j in range(3)]
-            shaped.append(tap[0] * now + tap[1] * one + tap[2] * two)
-        gate[rows, :] = shaped[0].astype(BF16)
-        kv[rows, :] = (shaped[1] * shaped[2]).astype(BF16)
+    shape(0, True)
 
     kv_plane = plane_exchange(kv, kv_xy, 1)
     arrived(kv_plane)

time: 113 us -> 112 us (level)
    pallas_call x1, Pallas kernels: 111 us -> 110 us  [local(): pl.pallas_call(kernel, out_shape=jax.ShapeDtypeStruct((SIDE, SIDE), BF16)...]
where the time goes in v6:
time: 112 us
  Pallas kernels  110 us (98%)
  local copies, waits for them, and re-layouts  1.57 us (1%)
    pallas_call x1, Pallas kernels, local(): pl.pallas_call(kernel, out_shape=jax.ShapeDtypeStruct((SIDE, SIDE), BF16)...  110 us

profile of v6, /device:TPU:128, one launch (start us, length us, event | category | flops | bytes accessed | tf_op | source)
XLA Modules:
  0.0 111.8 jit_solution(12255326636524371222)
XLA Ops:
  0.0 110.2 %hyena_operator.1 = bf16[256,256]{1,0:T(8,128)(2,1)} custom-call(bf16[3,256,256]{2,1,0:T(8,128)(2,1)} %feat_hbm.1, f32[3,3,256]{2,1,0:T(4,128)} %taps_hbm.1, bf16[256,256]{1,0:T(8,128)(2,1)} %filt_hbm.1, f32[1,256]{1,0:T(1,128)} %bitcast.1, bf16[256,4096]{1,0:T(8,128)(2,1)} %w_hbm.1), custom_call_target="tpu_custom_call" | custom-call | flops 4000000000 | bytes 3000000 | tf_op jit(solution)/shard_map/hyena_operator/pallas_call | solution.py:452
  110.2 1.6 %copy.7 = bf16[256,256]{1,0:T(8,128)(2,1)} copy(bf16[256,256]{1,0:T(8,128)(2,1)} %hyena_operator.1) | data formatting | bytes 262144

commit v7 on v6

--- a/solution.py
+++ b/solution.py
@@ -378,7 +378,8 @@
         def _():
             d = 7 - lax.div(n, PARTS)
             pass_on(
-                n, d, quarter == 0, (z_lo == 3) & (d > 4),
+                n, d, (quarter == 0) | ((z_lo == 2) & (d == 4)),
+                ((z_lo == 3) & (d > 4)) | ((z_lo == 1) & (d == 4)),
                 right_copy(n), right_jump(n, d), right_in, right_out,
             )
 
@@ -388,7 +389,8 @@
         def _():
             d = lax.div(m, PARTS)
             pass_on(
-                m, d, quarter == 3, (z_lo == 4) & (d < 3),
+                m, d, (quarter == 3) | ((z_lo == 5) & (d == 3)),
+                ((z_lo == 4) & (d < 3)) | ((z_lo == 6) & (d == 3)),
                 left_copy(m), left_jump(m, d), left_in, left_out,
             )
 
@@ -411,13 +413,13 @@
             left_copy(z_lo * PARTS + part).wait_recv()
         own[z_lo] = own[z_lo] + left_in[z_lo].astype(F32)
 
-    @pl.when(z_lo > 4)
+    @pl.when(z_lo > 3)
     def _():
         for part in range(PARTS):
             right_jump(part, z_lo).wait_recv()
         own[z_lo] = own[z_lo] + right_far[...].astype(F32)
 
-    @pl.when(z_lo < 3)
+    @pl.when(z_lo < 4)
     def _():
         for part in range(PARTS):
             left_jump(part, z_lo).wait_recv()

time: 112 us -> 114 us (1.018)
  the two profiles are of different devices: /device:TPU:128 before, /device:TPU:96 now
where the time goes in v7:
time: 114 us
  Pallas kernels  112 us (98%)
  local copies, waits for them, and re-layouts  1.57 us (1%)
    pallas_call x1, Pallas kernels, local(): pl.pallas_call(kernel, out_shape=jax.ShapeDtypeStruct((SIDE, SIDE), BF16)...  112 us

profile of v7, /device:TPU:96, one launch (start us, length us, event | category | flops | bytes accessed | tf_op | source)
XLA Modules:
  0.0 113.9 jit_solution(8827737550815513212)
XLA Ops:
  0.0 112.3 %hyena_operator.1 = bf16[256,256]{1,0:T(8,128)(2,1)} custom-call(bf16[3,256,256]{2,1,0:T(8,128)(2,1)} %feat_hbm.1, f32[3,3,256]{2,1,0:T(4,128)} %taps_hbm.1, bf16[256,256]{1,0:T(8,128)(2,1)} %filt_hbm.1, f32[1,256]{1,0:T(1,128)} %bitcast.1, bf16[256,4096]{1,0:T(8,128)(2,1)} %w_hbm.1), custom_call_target="tpu_custom_call" | custom-call | flops 4000000000 | bytes 3000000 | tf_op jit(solution)/shard_map/hyena_operator/pallas_call | solution.py:454
  112.3 1.6 %copy.7 = bf16[256,256]{1,0:T(8,128)(2,1)} copy(bf16[256,256]{1,0:T(8,128)(2,1)} %hyena_operator.1) | data formatting | bytes 262144
